TPU v7x, 256 devices: a whole 4x4x8 slice. The times are simulated.
256 devices in a mesh: dp: 8 (over x, core), expert: 32 (over z, y).
Axes of the slice: x: 4, y: 4, z: 8, core: 2. Of those that a mesh axis runs over, the one named last changes fastest.
Arguments:
- tokens: bfloat16 [32768, 2048], P(('dp', 'expert')), may hold values from -6 to 6
- expert_ids: int32 [32768, 8], P('dp'), may hold values from 0 to 31, all different within a row; in each aligned block of 128 rows (0 to 127, 128 to 255, ...) at most 48 rows name the same one
- gate_weights: float32 [32768, 8], P(('dp', 'expert')), may hold values from 0.25 to 2
- span_ids: int32 [8, 4096], P(None, 'expert'), may hold values from 0 to 63, as said below
- w_gate: bfloat16 [32, 2048, 768], P('expert'), may hold values from -0.125 to 0.125
- w_up: bfloat16 [32, 2048, 768], P('expert'), may hold values from -0.125 to 0.125
- w_down: bfloat16 [32, 768, 2048], P('expert'), may hold values from -0.21875 to 0.21875
- w_proj: bfloat16 [2048, 2560], P(None, 'dp'), may hold values from -0.125 to 0.125
- cotangent: bfloat16 [8, 2048, 2560], P(None, 'expert', 'dp'), may hold values from -0.046875 to 0.046875
Outputs:
- student: bfloat16 [8, 2048, 2560], P(None, 'expert', 'dp')
- grad_proj: float32 [2048, 2560], P('expert', 'dp')
Inputs may be any that keep to these rules, and one draw needn't show every extreme that they name: `expert_ids`: each row names 8 different experts. Within each aligned block of 128 rows (the tokens of one device) no expert is named by more than 48 rows, and in some blocks one expert is named by exactly 48. `span_ids`: each run of 128 entries of a row (one device's tokens) holds the span numbers 0 to 63 in order, never falling; each span has 1 to 4 tokens, and exactly one span of each run has 4.
All inputs are finite; a program needn't handle non-finite values.
Results may differ from a plain program's by a relative error of at most 0.015.
Values may be sent and summed in bfloat16 or wider, within the bound.
A program may use at most 128 MiB of HBM per device.

v0:
```python
import jax
import jax.numpy as jnp
from jax import lax
from jax.sharding import PartitionSpec as P


def slot_table(chosen, experts, cap):
    count, topk = chosen.shape
    hits = (chosen[:, :, None] == jnp.arange(experts, dtype=jnp.int32)[None, None, :]).astype(
        jnp.int32
    )
    per_token = jnp.sum(hits, axis=1)
    before = jnp.cumsum(per_token, axis=0) - per_token
    slot = jnp.sum(hits * before[:, None, :], axis=2)
    owners = jnp.repeat(jnp.arange(count, dtype=jnp.int32), topk)
    table = jnp.full((experts, cap), count, jnp.int32)
    table = table.at[chosen.reshape(-1), slot.reshape(-1)].set(owners)
    return (table, slot)


def local(tokens, expert_ids, gate_weights, span_ids, w_gate, w_up, w_down, w_proj, cotangent):
    groups = lax.axis_size("expert")
    member = lax.axis_index("expert")
    tok_dev, width = tokens.shape
    topk = expert_ids.shape[1]
    experts = groups * w_gate.shape[0]
    cap = min(tok_dev, 3 * tok_dev * topk // (2 * experts))
    own_ids = lax.dynamic_slice_in_dim(expert_ids, member * tok_dev, tok_dev, 0)
    zero_row = jnp.zeros((1, width), jnp.bfloat16)
    everyone = lax.all_gather(tokens, "expert", axis=0, tiled=True)
    id_blocks = expert_ids.reshape(groups, tok_dev, topk)
    tables, slots = jax.vmap(lambda chosen: slot_table(chosen, experts, cap))(id_blocks)
    mine = jnp.take(tables, member, axis=1)
    offsets = jnp.arange(groups, dtype=jnp.int32)[:, None] * tok_dev
    index = jnp.where(mine < tok_dev, mine + offsets, groups * tok_dev)
    padded = jnp.concatenate([everyone, zero_row], axis=0)
    arrived = jnp.take(padded, index, axis=0)
    rows = arrived.reshape(-1, width)
    gate = jnp.dot(rows, w_gate[0], preferred_element_type=jnp.float32)
    upper = jnp.dot(rows, w_up[0], preferred_element_type=jnp.float32)
    hidden = (jax.nn.silu(gate) * upper).astype(jnp.bfloat16)
    result = (
        jnp.dot(hidden, w_down[0], preferred_element_type=jnp.float32)
        .astype(jnp.bfloat16)
        .reshape(arrived.shape)
    )
    back = lax.all_to_all(result, "expert", split_axis=0, concat_axis=0, tiled=True)
    slot = jnp.take(slots, member, axis=0)
    flat = back.reshape(experts * cap, width)
    picked = jnp.take(flat, own_ids * cap + slot, axis=0)
    combined = jnp.einsum("tk,tkd->td", gate_weights, picked.astype(jnp.float32)).astype(
        jnp.bfloat16
    )
    replica = lax.axis_index("dp")
    spans_dev = tok_dev // 2
    local_ids = lax.dynamic_slice_in_dim(span_ids, replica, 1, 0)[0]
    onehot = local_ids[None, :] == jnp.arange(spans_dev, dtype=jnp.int32)[:, None]
    sums = jnp.dot(onehot.astype(jnp.bfloat16), combined, preferred_element_type=jnp.float32)
    counts = jnp.sum(onehot.astype(jnp.float32), axis=1)
    pooled = (sums / counts[:, None]).astype(jnp.bfloat16)
    pooled_all = lax.all_gather(pooled, "dp", axis=0, tiled=True)
    columns = w_proj.shape[1]
    student = jnp.dot(pooled_all, w_proj, preferred_element_type=jnp.float32).astype(jnp.bfloat16)
    student = student.reshape(cotangent.shape)
    cot_flat = cotangent.reshape(-1, columns)
    grad_proj = lax.psum_scatter(
        lax.dot_general(
            pooled_all, cot_flat, (((0,), (0,)), ((), ())), preferred_element_type=jnp.float32
        ),
        "expert",
        scatter_dimension=0,
        tiled=True,
    )
    return (student, grad_proj)


def solution(mesh):
    placed = (
        P(("dp", "expert"), None),
        P("dp", None),
        P(("dp", "expert"), None),
        P(None, "expert"),
        P("expert", None, None),
        P("expert", None, None),
        P("expert", None, None),
        P(None, "dp"),
        P(None, "expert", "dp"),
    )
    return jax.shard_map(
        local,
        mesh=mesh,
        in_specs=placed,
        out_specs=(P(None, "expert", "dp"), P("expert", "dp")),
        check_vma=False,
    )
```

profile of v0, /device:TPU:2, one launch (start us, length us, event | category | flops | bytes accessed | tf_op | source)
XLA Modules:
  0.0 645.8 jit_solution(17496606159923548585)
XLA Ops:
  8.7 2.8 copy.29
  11.6 2.3 convert_reduce_fusion
  13.8 3.8 copy.25
  17.7 1.9 fusion.13
  19.9 1.8 sub.7
  21.7 3.5 copy.27
  25.2 2.4 select_reduce_fusion
  27.6 1.0 copy.30
  28.6 1.2 copy.31
  29.8 3.4 reshape_reshape.3
  33.3 0.9 compare_select_fusion
  35.2 120.4 %scatter_custom_fusion = s32[49152]{0:T(1024)S(1)} fusion(s32[32768]{0:T(1024)} %bitcast.63, s32[32768]{0:T(1024)} %bitcast.62, s32[]{:T(128)} %constant.56.clone.1), kind=kCustom, calls=%fused_computation.27 | custom fusion | bytes 197120
  155.7 1.0 reshape.230
  156.7 0.9 broadcast_select_fusion.1
  157.9 13.9 %concatenate.7 = bf16[4097,2048]{1,0:T(8,128)(2,1)} pad(bf16[4096,2048]{1,0:T(8,128)(2,1)} %all-gather.3.cloned.1.call-done, bf16[]{:T(256)} %constant.88.clone.1), padding=0_1x0_0 | pad | bytes 33558528 | tf_op jit(solution)/shard_map/concatenate | solution.py:36
  171.7 20.7 %gather_fusion = bf16[1536,2048]{1,0:T(8,128)(2,1)} fusion(bf16[4097,2048]{1,0:T(8,128)(2,1)} %concatenate.7, s32[2048]{0:T(1024)S(1)} %pad_clamp_fusion), kind=kCustom, calls=%fused_computation | custom fusion | bytes 12589056 | tf_op jit(solution)/shard_map/jit(_take)/gather | solution.py:37
  192.4 3.6 broadcast_select_fusion
  196.1 5.2 fusion.4
  201.3 5.6 multiply_convert_fusion
  207.0 7.3 %convolution_convert_fusion = bf16[1536,2048]{1,0:T(8,128)(2,1)} fusion(bf16[1536,768]{1,0:T(8,128)(2,1)S(1)} %multiply_convert_fusion, bf16[1,768,2048]{2,1,0:T(8,128)(2,1)S(1)} %copy-done), kind=kOutput, calls=%fused_computation.3 | convolution fusion | flops 4834983936 | bytes 11796480 | tf_op jit(solution)/shard_map/dot_general | solution.py:43
  214.2 11.8 %all-to-all-start = ((bf16[32,48,2048]{2,1,0:T(8,128)(2,1)}), bf16[32,48,2048]{2,1,0:T(8,128)(2,1)}, u32[]{:S(2)}, u32[]{:S(2)}) async-start(bf16[32,48,2048]{2,1,0:T(8,128)(2,1)} %bitcast.52), calls=%async_computation | async-start | bytes 12582912 | tf_op jit(solution)/shard_map/all_to_all | solution.py:47
  226.1 0.8 copy.36
  227.9 0.7 fusion.11
  229.2 138.1 %all-to-all-done = bf16[32,48,2048]{2,1,0:T(8,128)(2,1)} async-done(((bf16[32,48,2048]{2,1,0:T(8,128)(2,1)}), bf16[32,48,2048]{2,1,0:T(8,128)(2,1)}, u32[]{:S(2)}, u32[]{:S(2)}) %all-to-all-start) | async-done | bytes 6291488 | tf_op jit(solution)/shard_map/all_to_all | solution.py:47
  367.4 12.4 %gather_fusion.1 = bf16[1024,2048]{1,0:T(8,128)(2,1)} fusion(bf16[1536,2048]{1,0:T(8,128)(2,1)} %bitcast.12, s32[1024]{0:T(1024)S(1)} %broadcast_clamp_fusion), kind=kCustom, calls=%fused_computation.1 | custom fusion | bytes 8392704 | tf_op jit(solution)/shard_map/jit(_take)/gather | solution.py:50
  379.8 3.6 fusion
  383.4 1.1 fusion.6
  384.6 29.4 %all-gather.5.cloned.1.call-done = bf16[512,2048]{1,0:T(8,128)(2,1)} async-done(((bf16[64,2048]{1,0:T(8,128)(2,1)}), bf16[512,2048]{1,0:T(8,128)(2,1)}) %all-gather.5.cloned.1.call-update) | async-done | bytes 2097168 | tf_op jit(solution)/shard_map/all_gather | solution.py:61
  414.0 4.5 fusion.14
  418.6 2.8 convolution_convert_fusion.1
  421.4 0.9 copy.35
  422.3 216.9 %reduce-scatter.2.cloned.1.call-done = f32[64,320]{1,0:T(8,128)} async-done(((f32[2048,320]{1,0:T(8,128)}), f32[64,320]{1,0:T(8,128)}) %reduce-scatter.2.cloned.1.call-update) | async-done | bytes 81936 | tf_op jit(solution)/shard_map/reduce_scatter | solution.py:66
  (53 shorter events, 4.9 us)
Async XLA Ops:
  7.2 199.8 %copy-start = (bf16[1,768,2048]{2,1,0:T(8,128)(2,1)S(1)}, bf16[1,768,2048]{2,1,0:T(8,128)(2,1)}, u32[]{:S(2)}) copy-start(bf16[1,768,2048]{2,1,0:T(8,128)(2,1)} %param.15) | copy-start | bytes 9437188
  7.2 150.7 %all-gather.3.cloned.1.call-start = ((), (), s32[]{:S(2)}) async-start(), calls=%async_computation.2 | async-start | bytes 17301504 | tf_op jit(solution)/shard_map/all_gather | solution.py:30
  17.7 2.2 copy-start.1
  19.9 5.3 copy-start.2
  21.7 12.6 %copy-start.7 = (s32[3]{0:T(128)S(1)}, s32[3]{0:T(128)}, u32[]{:S(2)}) copy-start(s32[3]{0:T(128)} %constant.99) | copy-start | bytes 40
  21.7 12.7 %copy-start.6 = (s32[3]{0:T(128)S(1)}, s32[3]{0:T(128)}, u32[]{:S(2)}) copy-start(s32[3]{0:T(128)} %constant.102) | copy-start | bytes 40
  27.6 7.6 %copy-start.3 = (s32[32,128,8]{1,2,0:T(8,128)}, s32[32,128,8]{1,2,0:T(8,128)S(1)}, u32[]{:S(2)}) copy-start(s32[32,128,8]{1,2,0:T(8,128)S(1)} %select_reduce_fusion) | copy-start | bytes 393220
  192.4 3.7 copy-start.8
  196.1 5.2 copy-start.9
  214.2 11.9 %copy-start.5 = (f32[128,8]{0,1:T(8,128)S(1)}, f32[128,8]{0,1:T(8,128)}, u32[]{:S(2)}) copy-start(f32[128,8]{0,1:T(8,128)} %param.11) | copy-start | bytes 12292
  214.2 153.1 %all-to-all-start = ((bf16[32,48,2048]{2,1,0:T(8,128)(2,1)}), bf16[32,48,2048]{2,1,0:T(8,128)(2,1)}, u32[]{:S(2)}, u32[]{:S(2)}) async-start(bf16[32,48,2048]{2,1,0:T(8,128)(2,1)} %bitcast.52), calls=%async_computation | async-start | bytes 12582912 | tf_op jit(solution)/shard_map/all_to_all | solution.py:47
  226.1 188.0 %all-gather.5.cloned.1.call-start = ((), (), s32[]{:S(2)}) async-start(), calls=%async_computation.3 | async-start | bytes 2359296 | tf_op jit(solution)/shard_map/all_gather | solution.py:61
  228.6 138.8 %copy-start.10 = (s32[128]{0:T(128)}, s32[128]{0:T(128)S(1)}, u32[]{:S(2)}) copy-start(s32[128]{0:T(128)S(1)} %fusion.11) | copy-start | bytes 1540
  379.8 3.6 copy-start.11
  379.8 3.6 copy-start.12
  379.8 34.2 %copy-start.4 = (bf16[8,64,320]{2,1,0:T(8,128)(2,1)S(1)}, bf16[8,64,320]{2,1,0:T(8,128)(2,1)}, u32[]{:S(2)}) copy-start(bf16[8,64,320]{2,1,0:T(8,128)(2,1)} %param.17) | copy-start | bytes 983044
  384.6 254.7 %reduce-scatter.2.cloned.1.call-start = ((), (), s32[]{:S(2)}) async-start(), calls=%async_computation.4 | async-start | bytes 3244032 | tf_op jit(solution)/shard_map/reduce_scatter | solution.py:66
Sparse Core Ops, SparseCore 0:
  10.6 143.5 all-gather.2
  384.7 29.2 all-gather.4
  418.7 220.5 reduce-scatter.1
where the time goes:
time: 647 us; the launch traced here: 646 us
  waiting for transfers between devices  385 us (60%)
  local copies, waits for them, and re-layouts  189 us (29%)
  matrix products  30.2 us (5%)
  other arithmetic  15.6 us (2%)
  between operations  14 us (2%)
  starting transfers between devices  11.9 us (2%)
    reduce_scatter x1, waiting for transfers between devices, local(): lax.psum_scatter(lax.dot_general(pooled_all, cot_flat, (((0,), (0,)), (()...  217 us
    all_to_all x1, waiting for transfers between devices, local(): lax.all_to_all(result, 'expert', split_axis=0, concat_axis=0, tiled=True)  138 us
    unnamed x33, local copies, waits for them, and re-layouts  126 us
    all_gather x1, waiting for transfers between devices, local(): pooled_all = lax.all_gather(pooled, 'dp', axis=0, tiled=True)  29.4 us
    gather x1, local copies, waits for them, and re-layouts, local(): arrived = jnp.take(padded, index, axis=0)  20.7 us
    concatenate x1, local copies, waits for them, and re-layouts, local(): padded = jnp.concatenate([everyone, zero_row], axis=0)  13.9 us
  transfers between devices with their start and end apart: 4, of which 3 were waited for; matrix products, arithmetic and copies ran while one was open for 24% of the time, Pallas kernels for 0%

commit v1 on v0

v1 whole, which is shorter than its diff:
```python
import jax
import jax.numpy as jnp
from jax import lax
from jax.experimental import pallas as pl
from jax.experimental.pallas import tpu as pltpu
from jax.sharding import PartitionSpec as P

MESH = pl.DeviceIdType.MESH
NZ, NY = 8, 4
CAP = 48
DELTA = (0, -1, 1, -2, 2, -3, 3, 4)
PAIR = (0, 2, 1, 4, 3, 6, 5, 7)
RETURN_ORDER = (5, 6, 7, 3, 4, 1, 2, 0)


def place():
    d = lax.axis_index("dp")
    e = lax.axis_index("expert")
    return d, e // NY, lax.rem(e, NY)


def at_z(d, z, y, dz):
    return (d, lax.rem(z + NZ + dz, NZ) * NY + y)


def at_y(d, z, y, dy):
    return (d, z * NY + lax.rem(y + NY + dy, NY))


def moe_kernel(
    tokens, ids_hbm, gates, spans, wg_hbm, wu_hbm, wd_hbm, pooled,
    ids, wg, wu, wd, slot_t, gate_t, meta_out, meta, zbuf, sbuf, xbuf, hid, rbuf, bbuf,
    qbuf, msg, got, load_sem, meta_ss, meta_rs, z_ss, z_rs, y_ss, y_rs, b_ss, b_rs, c_ss, c_rs,
):
    d, z, y = place()
    e = z * NY + y
    tok, width = tokens.shape
    ff = wg.shape[1]
    spn = pooled.shape[0]
    half_t, half_s = tok // 2, spn // 2

    barrier = pltpu.get_barrier_semaphore()
    for dz in DELTA[1:]:
        pl.semaphore_signal(barrier, inc=1, device_id=at_z(d, z, y, dz), device_id_type=MESH)
    for dy in range(1, NY):
        pl.semaphore_signal(barrier, inc=1, device_id=at_y(d, z, y, dy), device_id_type=MESH)
    ids_copy = pltpu.make_async_copy(ids_hbm.at[pl.ds(e * tok, tok)], ids, load_sem.at[3])
    ids_copy.start()
    loads = [
        pltpu.make_async_copy(src.at[0], dst, load_sem.at[n])
        for n, (src, dst) in enumerate(((wg_hbm, wg), (wu_hbm, wu), (wd_hbm, wd)))
    ]
    for load in loads:
        load.start()
    pl.semaphore_wait(barrier, NZ - 1 + NY - 1)

    def remote(src, dst, ss, rs, dev):
        return pltpu.make_async_remote_copy(
            src_ref=src, dst_ref=dst, send_sem=ss, recv_sem=rs, device_id=dev, device_id_type=MESH
        )

    pending = []

    def z_send(src, dst, s, dz):
        copy = remote(src, dst, z_ss.at[s], z_rs.at[s], at_z(d, z, y, dz))
        copy.start()
        pending.append(copy)

    z_send(tokens, zbuf.at[1], 1, 1)
    z_send(tokens, zbuf.at[2], 2, -1)

    ids_copy.wait()
    lanes = lax.broadcasted_iota(jnp.int32, (tok, 128), 1)
    taken = jnp.zeros((tok, 128), jnp.float32)
    weight = jnp.zeros((tok, 128), jnp.float32)
    for k in range(ids.shape[1]):
        named = ids[:, k : k + 1] == lanes
        taken = taken + jnp.where(named, 1.0, 0.0)
        weight = weight + jnp.where(named, gates[:, k : k + 1], 0.0)
    rows = lax.broadcasted_iota(jnp.int32, (tok, tok), 0)
    cols = lax.broadcasted_iota(jnp.int32, (tok, tok), 1)
    earlier = jnp.where(cols < rows, 1.0, 0.0).astype(jnp.bfloat16)
    before = jnp.dot(earlier, taken.astype(jnp.bfloat16), preferred_element_type=jnp.float32)
    slot_t[...] = jnp.transpose(jnp.where(taken > 0.0, before, -1.0))
    gate_t[...] = jnp.transpose(weight)
    own_span = spans[pl.ds(d, 1), :].astype(jnp.float32)
    meta_copies = []
    for i in range(NZ):
        there = lax.rem(z + NZ + DELTA[i], NZ) * NY
        for j in range(NY):
            row = there + lax.rem(y + j, NY)
            slab = meta if i == 0 else meta_out
            slab[i, j, 0:1, :] = slot_t[pl.ds(row, 1), :]
            slab[i, j, 1:2, :] = gate_t[pl.ds(row, 1), :]
            slab[i, j, 2:3, :] = own_span
        if i > 0:
            copy = remote(
                meta_out.at[i], meta.at[PAIR[i]], meta_ss.at[i], meta_rs.at[PAIR[i]],
                at_z(d, z, y, DELTA[i]),
            )
            copy.start()
            meta_copies.append(copy)

    def meta_wait(i):
        if i > 0:
            remote(meta_out.at[i], meta.at[i], meta_ss.at[i], meta_rs.at[i], (d, e)).wait_recv()

    slots = lax.broadcasted_iota(jnp.int32, (CAP, tok), 0).astype(jnp.float32)

    def onehot(i, j):
        return jnp.where(meta[i, j, 0:1, :] == slots, 1.0, 0.0)

    y_copies = {}

    def dispatch(i):
        block = tokens if i == 0 else zbuf.at[i]
        pick = jnp.concatenate([onehot(i, j) for j in range(NY)], axis=0).astype(jnp.bfloat16)
        tile = 512

        def body(n, carry):
            at = pl.ds(pl.multiple_of(n * tile, tile), tile)
            out = jnp.dot(pick, block[:, at], preferred_element_type=jnp.float32)
            out = out.astype(jnp.bfloat16)
            xbuf[i, 0:CAP, at] = out[0:CAP]
            sbuf[i, :, at] = out[CAP:]
            return carry

        lax.fori_loop(0, width // tile, body, 0)
        for j in range(1, NY):
            back = NY - j
            copy = remote(
                sbuf.at[i, pl.ds((j - 1) * CAP, CAP)], xbuf.at[i, pl.ds(back * CAP, CAP)],
                y_ss.at[i, j], y_rs.at[i, back], at_y(d, z, y, j),
            )
            copy.start()
            y_copies[i, j] = copy

    def ffn(i):
        for j in range(1, NY):
            remote(
                sbuf.at[i, pl.ds((j - 1) * CAP, CAP)], xbuf.at[i, pl.ds(j * CAP, CAP)],
                y_ss.at[i, j], y_rs.at[i, j], (d, e),
            ).wait_recv()
        wide = 256

        def up(n, carry):
            at = pl.ds(pl.multiple_of(n * wide, wide), wide)
            x = xbuf[i]
            g = jnp.dot(x, wg[:, at], preferred_element_type=jnp.float32)
            u = jnp.dot(x, wu[:, at], preferred_element_type=jnp.float32)
            hid[:, at] = (g / (1.0 + jnp.exp(-g)) * u).astype(jnp.bfloat16)
            return carry

        lax.fori_loop(0, ff // wide, up, 0)

        def down(n, carry):
            at = pl.ds(pl.multiple_of(n * wide, wide), wide)
            out = jnp.dot(hid[...], wd[:, at], preferred_element_type=jnp.float32)
            out = out.astype(jnp.bfloat16)
            bbuf[i, 0:CAP, at] = out[0:CAP]
            rbuf[i, :, at] = out[CAP:]
            return carry

        lax.fori_loop(0, width // wide, down, 0)

    b_copies = {}

    def give_back(i):
        for j in range(1, NY):
            back = NY - j
            copy = remote(
                rbuf.at[i, pl.ds((j - 1) * CAP, CAP)], bbuf.at[i, pl.ds(back * CAP, CAP)],
                b_ss.at[i, j], b_rs.at[i, back], at_y(d, z, y, j),
            )
            copy.start()
            b_copies[i, j] = copy

    span_rows = lax.broadcasted_iota(jnp.int32, (spn, tok), 0).astype(jnp.float32)
    last = (((1,), (1,)), ((), ()))

    def pool(i):
        for j in range(1, NY):
            remote(
                rbuf.at[i, pl.ds((j - 1) * CAP, CAP)], bbuf.at[i, pl.ds(j * CAP, CAP)],
                b_ss.at[i, j], b_rs.at[i, j], (d, e),
            ).wait_recv()
        high, low = [], []
        for j in range(NY):
            take = onehot(i, j).astype(jnp.bfloat16)
            share = jnp.where(meta[i, j, 2:3, :] == span_rows, meta[i, j, 1:2, :], 0.0)
            top = share.astype(jnp.bfloat16)
            rest = (share - top.astype(jnp.float32)).astype(jnp.bfloat16)
            high.append(lax.dot_general(top, take, last, preferred_element_type=jnp.float32))
            low.append(lax.dot_general(rest, take, last, preferred_element_type=jnp.float32))
        high = jnp.concatenate(high, axis=1).astype(jnp.bfloat16)
        low = jnp.concatenate(low, axis=1).astype(jnp.bfloat16)
        both = jnp.concatenate([high, low], axis=0)
        tile = 512

        def body(n, carry):
            at = pl.ds(pl.multiple_of(n * tile, tile), tile)
            out = jnp.dot(both, bbuf[i, :, at], preferred_element_type=jnp.float32)
            qbuf[i, :, at] = out[:spn] + out[spn:]
            return carry

        lax.fori_loop(0, width // tile, body, 0)

    chain = []

    def pass_on(way, hop, i):
        if hop == NZ // 2:
            part = pl.ds(way * half_s, half_s)
            msg[way, hop - 1, part, :] = qbuf[i, part, :].astype(jnp.bfloat16)
        else:
            src = remote_got(way, hop)
            src.wait_recv()
            if hop == NZ // 2 - 1:
                part, other = pl.ds(way * half_s, half_s), pl.ds((1 - way) * half_s, half_s)
                msg[way, hop - 1, part, :] = (
                    qbuf[i, part, :] + got[way, hop, part, :].astype(jnp.float32)
                ).astype(jnp.bfloat16)
                msg[way, hop - 1, other, :] = qbuf[i, other, :].astype(jnp.bfloat16)
            else:
                msg[way, hop - 1] = (
                    qbuf[i] + got[way, hop].astype(jnp.float32)
                ).astype(jnp.bfloat16)
        copy = remote(
            chain_part(msg, way, hop - 1), chain_part(got, way, hop - 1),
            c_ss.at[way, hop - 1], c_rs.at[way, hop - 1], at_z(d, z, y, 1 - 2 * way),
        )
        copy.start()
        chain.append(copy)

    def chain_part(buf, way, n):
        if n == NZ // 2 - 1:
            return buf.at[way, n, pl.ds(way * half_s, half_s)]
        return buf.at[way, n]

    def remote_got(way, n):
        return remote(
            chain_part(msg, way, n), chain_part(got, way, n), c_ss.at[way, n], c_rs.at[way, n], (d, e)
        )

    meta_wait(0)
    dispatch(0)

    def z_recv(s, part=None):
        dst = zbuf.at[s] if part is None else zbuf.at[7, pl.ds(part * half_t, half_t)]
        n = s if part is None else 7 + part
        remote(dst, dst, z_ss.at[n], z_rs.at[n], (d, e)).wait_recv()

    for p in (1, 2, 3):
        a, b = 2 * p - 1, 2 * p
        z_recv(a)
        if p < 3:
            z_send(zbuf.at[a], zbuf.at[a + 2], a + 2, 1)
        else:
            part = pl.ds(0, half_t)
            z_send(zbuf.at[a, part], zbuf.at[7, part], 7, 1)
        z_recv(b)
        if p < 3:
            z_send(zbuf.at[b], zbuf.at[b + 2], b + 2, -1)
        else:
            part = pl.ds(half_t, half_t)
            z_send(zbuf.at[b, part], zbuf.at[7, part], 8, -1)
        for i in (a, b):
            meta_wait(i)
            dispatch(i)
        if p == 1:
            for load in loads:
                load.wait()
            ffn(0)
        if p == 3:
            ffn(1)
            ffn(2)
    z_recv(7, 0)
    z_recv(7, 1)
    meta_wait(7)
    dispatch(7)
    for i in (3, 4, 5, 6):
        ffn(i)
    give_back(5)
    give_back(6)
    ffn(7)
    give_back(7)
    for n, i in enumerate(RETURN_ORDER):
        pool(i)
        if n + 3 < NZ:
            give_back(RETURN_ORDER[n + 3])
        if i == 7:
            pass_on(0, 4, 7)
            pass_on(1, 4, 7)
            pass_on(0, 3, 6)
            pass_on(1, 3, 5)
        if i == 4:
            pass_on(0, 2, 4)
            pass_on(1, 2, 3)
        if i == 2:
            pass_on(0, 1, 2)
            pass_on(1, 1, 1)
    count = jnp.sum(jnp.where(own_span == span_rows, 1.0, 0.0), axis=1, keepdims=True)
    remote_got(0, 0).wait_recv()
    remote_got(1, 0).wait_recv()
    total = qbuf[0] + got[0, 0].astype(jnp.float32) + got[1, 0].astype(jnp.float32)
    pooled[...] = (total / count).astype(jnp.bfloat16)
    for copy in pending + meta_copies + list(y_copies.values()) + list(b_copies.values()) + chain:
        copy.wait_send()


def moe(tokens, expert_ids, gate_weights, span_ids, w_gate, w_up, w_down):
    tok, width = tokens.shape
    ff = w_gate.shape[2]
    spn = tok // 2
    vmem = pl.BlockSpec(memory_space=pltpu.VMEM)
    hbm = pl.BlockSpec(memory_space=pl.ANY)
    bf, f32 = jnp.bfloat16, jnp.float32
    dma = pltpu.SemaphoreType.DMA
    return pl.pallas_call(
        moe_kernel,
        out_shape=jax.ShapeDtypeStruct((spn, width), bf),
        in_specs=[vmem, hbm, vmem, vmem, hbm, hbm, hbm],
        out_specs=vmem,
        scratch_shapes=[
            pltpu.VMEM((tok, expert_ids.shape[1]), jnp.int32),
            pltpu.VMEM((width, ff), bf),
            pltpu.VMEM((width, ff), bf),
            pltpu.VMEM((ff, width), bf),
            pltpu.VMEM((128, tok), f32),
            pltpu.VMEM((128, tok), f32),
            pltpu.VMEM((NZ, NY, 8, tok), f32),
            pltpu.VMEM((NZ, NY, 8, tok), f32),
            pltpu.VMEM((NZ, tok, width), bf),
            pltpu.VMEM((NZ, (NY - 1) * CAP, width), bf),
            pltpu.VMEM((NZ, NY * CAP, width), bf),
            pltpu.VMEM((NY * CAP, ff), bf),
            pltpu.VMEM((NZ, (NY - 1) * CAP, width), bf),
            pltpu.VMEM((NZ, NY * CAP, width), bf),
            pltpu.VMEM((NZ, spn, width), f32),
            pltpu.VMEM((2, NZ // 2, spn, width), bf),
            pltpu.VMEM((2, NZ // 2, spn, width), bf),
            dma((4,)),
            dma((NZ,)), dma((NZ,)),
            dma((NZ + 1,)), dma((NZ + 1,)),
            dma((NZ, NY)), dma((NZ, NY)),
            dma((NZ, NY)), dma((NZ, NY)),
            dma((2, NZ // 2)), dma((2, NZ // 2)),
        ],
        compiler_params=pltpu.CompilerParams(
            collective_id=0, has_side_effects=True, vmem_limit_bytes=60 * 2**20
        ),
    )(tokens, expert_ids, gate_weights, span_ids, w_gate, w_up, w_down)


def local(tokens, expert_ids, gate_weights, span_ids, w_gate, w_up, w_down, w_proj, cotangent):
    pooled = moe(tokens, expert_ids, gate_weights, span_ids, w_gate, w_up, w_down)
    pooled_all = lax.all_gather(pooled, "dp", axis=0, tiled=True)
    columns = w_proj.shape[1]
    student = jnp.dot(pooled_all, w_proj, preferred_element_type=jnp.float32).astype(jnp.bfloat16)
    student = student.reshape(cotangent.shape)
    cot_flat = cotangent.reshape(-1, columns)
    grad_proj = lax.psum_scatter(
        lax.dot_general(
            pooled_all, cot_flat, (((0,), (0,)), ((), ())), preferred_element_type=jnp.float32
        ),
        "expert",
        scatter_dimension=0,
        tiled=True,
    )
    return (student, grad_proj)


def solution(mesh):
    placed = (
        P(("dp", "expert"), None),
        P("dp", None),
        P(("dp", "expert"), None),
        P(None, "expert"),
        P("expert", None, None),
        P("expert", None, None),
        P("expert", None, None),
        P(None, "dp"),
        P(None, "expert", "dp"),
    )
    return jax.shard_map(
        local,
        mesh=mesh,
        in_specs=placed,
        out_specs=(P(None, "expert", "dp"), P("expert", "dp")),
        check_vma=False,
    )
```

time: 647 us -> 424 us (0.66)
  local copies, waits for them, and re-layouts: 189 us -> 7.15 us
  Pallas kernels: 0 us -> 157 us
  waiting for transfers between devices: 385 us -> 239 us
  matrix products: 30.2 us -> 6.14 us
  other arithmetic: 15.6 us -> 0 us
  starting transfers between devices: 11.9 us -> 0.08 us
    pallas_call x0 -> x1, Pallas kernels: none -> 157 us  [moe(): pl.pallas_call(moe_kernel, out_shape=jax.ShapeDtypeStruct((spn, width), b...]
    all_to_all x1 -> x0, waiting for transfers between devices: 138 us -> none  [local(): lax.all_to_all(result, 'expert', split_axis=0, concat_axis=0, tiled=True)]
    unnamed x33 -> x10, local copies, waits for them, and re-layouts: 126 us -> 5.26 us
    gather x2 -> x0, local copies, waits for them, and re-layouts: 33 us -> none  [the longest x1 20.7 us: local(): arrived = jnp.take(padded, index, axis=0)]
    dot_general x5 -> x0, matrix products: 22.8 us -> none  [the longest x1 7.26 us: local(): jnp.dot(hidden, w_down[0], preferred_element_type=jnp.float32)]
    concatenate x1 -> x0, local copies, waits for them, and re-layouts: 13.9 us -> none  [local(): padded = jnp.concatenate([everyone, zero_row], axis=0)]
    all_to_all x1 -> x0, starting transfers between devices: 11.8 us -> none  [local(): lax.all_to_all(result, 'expert', split_axis=0, concat_axis=0, tiled=True)]
  transfers between devices with their start and end apart: 4 -> 2, of which waited for: 3 -> 2; matrix products, arithmetic and copies ran while one was open for 24% -> 1% of each run, Pallas kernels for 0% -> 0%
where the time goes in v1:
time: 424 us; the launch traced here: 423 us
  waiting for transfers between devices  239 us (56%)
  Pallas kernels  157 us (37%)
  between operations  14.1 us (3%)
  local copies, waits for them, and re-layouts  7.15 us (2%)
  matrix products  6.14 us (1%)
    reduce_scatter x1, waiting for transfers between devices, local(): lax.psum_scatter(lax.dot_general(pooled_all, cot_flat, (((0,), (0,)), (()...  216 us
    pallas_call x1, Pallas kernels, moe(): pl.pallas_call(moe_kernel, out_shape=jax.ShapeDtypeStruct((spn, width), b...  157 us
    all_gather x1, waiting for transfers between devices, local(): pooled_all = lax.all_gather(pooled, 'dp', axis=0, tiled=True)  23.3 us
  transfers between devices with their start and end apart: 2, of which 2 were waited for; matrix products, arithmetic and copies ran while one was open for 1% of the time, Pallas kernels for 0%

profile of v1, /device:TPU:2, one launch (start us, length us, event | category | flops | bytes accessed | tf_op | source)
XLA Modules:
  0.0 423.3 jit_solution(5339654567137335766)
XLA Ops:
  7.2 0.0 copy-start
  7.2 0.0 copy-start.3
  7.2 0.0 all-gather.2.cloned.1.call-start
  7.2 3.0 copy.14.ids_hbm
  10.2 0.0 copy-done.3
  10.2 0.7 copy.15.gates
  10.9 0.0 copy-start.2
  10.9 156.8 %shard_map.104 = bf16[64,2048]{1,0:T(8,128)(2,1)} custom-call(bf16[128,2048]{1,0:T(8,128)(2,1)} %tokens.1, s32[4096,8]{1,0:T(8,128)} %copy.14.ids_hbm, f32[128,8]{1,0:T(8,128)} %copy.15.gates, s32[8,128]{1,0:T(8,128)} %spans.1, bf16[1,2048,768]{2,1,0:T(8,128)(2,1)} %wg_hbm.1, bf16[1,2048,768]{2,1,0:T(8,128)(2,1)} %wu_hbm.1, bf16[1,768,2048]{2,1,0:T(8,128)(2,1)} %wd_hbm.1), custom_call_target="tpu_custom_call" | custom-call | tf_op jit(solution)/shard_map/pallas_call | solution.py:318
  167.7 0.0 all-gather.2.cloned.1.call-update
  167.7 0.0 reduce-scatter.2.cloned.1.call-start
  167.8 23.3 %all-gather.2.cloned.1.call-done = bf16[512,2048]{1,0:T(8,128)(2,1)} async-done(((bf16[64,2048]{1,0:T(8,128)(2,1)}), bf16[512,2048]{1,0:T(8,128)(2,1)}) %all-gather.2.cloned.1.call-update) | async-done | bytes 2097168 | tf_op jit(solution)/shard_map/all_gather | solution.py:356
  191.1 0.0 copy-done.2
  191.1 4.5 %fusion = f32[2048,320]{1,0:T(8,128)} fusion(bf16[512,2048]{1,0:T(8,128)(2,1)} %all-gather.2.cloned.1.call-done, bf16[512,320]{1,0:T(8,128)(2,1)S(1)} %bitcast.7), kind=kOutput, calls=%fused_computation.1 | convolution fusion | flops 671088640 | bytes 5046272 | tf_op jit(solution)/shard_map/dot_general | solution.py:362
  195.6 0.0 copy-start.1
  195.6 0.0 reduce-scatter.2.cloned.1.call-update
  195.6 0.0 copy-done
  195.7 1.6 copy-done.1
  197.2 1.6 convolution_convert_fusion
  198.8 1.9 copy.16
  200.7 215.8 %reduce-scatter.2.cloned.1.call-done = f32[64,320]{1,0:T(8,128)} async-done(((f32[2048,320]{1,0:T(8,128)}), f32[64,320]{1,0:T(8,128)}) %reduce-scatter.2.cloned.1.call-update) | async-done | bytes 81936 | tf_op jit(solution)/shard_map/reduce_scatter | solution.py:361
Async XLA Ops:
  7.2 188.5 %copy-start = (bf16[2048,320]{0,1:T(8,128)(2,1)S(1)}, bf16[2048,320]{0,1:T(8,128)(2,1)}, u32[]{:S(2)}) copy-start(bf16[2048,320]{0,1:T(8,128)(2,1)} %param.16) | copy-start | bytes 3932164
  7.2 3.0 copy-start.3
  7.2 183.9 %all-gather.2.cloned.1.call-start = ((), (), s32[]{:S(2)}) async-start(), calls=%async_computation.1 | async-start | bytes 2359296 | tf_op jit(solution)/shard_map/all_gather | solution.py:356
  10.9 180.2 %copy-start.2 = (bf16[8,64,320]{2,1,0:T(8,128)(2,1)S(1)}, bf16[8,64,320]{2,1,0:T(8,128)(2,1)}, u32[]{:S(2)}) copy-start(bf16[8,64,320]{2,1,0:T(8,128)(2,1)} %param.17) | copy-start | bytes 983044
  167.7 248.8 %reduce-scatter.2.cloned.1.call-start = ((), (), s32[]{:S(2)}) async-start(), calls=%async_computation.2 | async-start | bytes 3244032 | tf_op jit(solution)/shard_map/reduce_scatter | solution.py:361
  195.6 1.6 copy-start.1
Sparse Core Ops, SparseCore 0:
  167.9 23.1 all-gather.1
  195.8 220.6 reduce-scatter.1

commit v2 on v1

--- a/solution.py
+++ b/solution.py
@@ -44,7 +44,7 @@
         pl.semaphore_signal(barrier, inc=1, device_id=at_z(d, z, y, dz), device_id_type=MESH)
     for dy in range(1, NY):
         pl.semaphore_signal(barrier, inc=1, device_id=at_y(d, z, y, dy), device_id_type=MESH)
-    ids_copy = pltpu.make_async_copy(ids_hbm.at[pl.ds(e * tok, tok)], ids, load_sem.at[3])
+    ids_copy = pltpu.make_async_copy(ids_hbm.at[:, pl.ds(pl.multiple_of(e * tok, tok), tok)], ids, load_sem.at[3])
     ids_copy.start()
     loads = [
         pltpu.make_async_copy(src.at[0], dst, load_sem.at[n])
@@ -70,19 +70,20 @@
     z_send(tokens, zbuf.at[2], 2, -1)
 
     ids_copy.wait()
-    lanes = lax.broadcasted_iota(jnp.int32, (tok, 128), 1)
-    taken = jnp.zeros((tok, 128), jnp.float32)
-    weight = jnp.zeros((tok, 128), jnp.float32)
-    for k in range(ids.shape[1]):
-        named = ids[:, k : k + 1] == lanes
+    experts = NZ * NY
+    number = lax.broadcasted_iota(jnp.int32, (experts, tok), 0)
+    taken = jnp.zeros((experts, tok), jnp.float32)
+    weight = jnp.zeros((experts, tok), jnp.float32)
+    for k in range(ids.shape[0]):
+        named = ids[k : k + 1, :] == number
         taken = taken + jnp.where(named, 1.0, 0.0)
-        weight = weight + jnp.where(named, gates[:, k : k + 1], 0.0)
+        weight = weight + jnp.where(named, gates[k : k + 1, :], 0.0)
     rows = lax.broadcasted_iota(jnp.int32, (tok, tok), 0)
     cols = lax.broadcasted_iota(jnp.int32, (tok, tok), 1)
-    earlier = jnp.where(cols < rows, 1.0, 0.0).astype(jnp.bfloat16)
-    before = jnp.dot(earlier, taken.astype(jnp.bfloat16), preferred_element_type=jnp.float32)
-    slot_t[...] = jnp.transpose(jnp.where(taken > 0.0, before, -1.0))
-    gate_t[...] = jnp.transpose(weight)
+    earlier = jnp.where(rows < cols, 1.0, 0.0).astype(jnp.bfloat16)
+    before = jnp.dot(taken.astype(jnp.bfloat16), earlier, preferred_element_type=jnp.float32)
+    slot_t[...] = jnp.where(taken > 0.0, before, -1.0)
+    gate_t[...] = weight
     own_span = spans[pl.ds(d, 1), :].astype(jnp.float32)
     meta_copies = []
     for i in range(NZ):
@@ -321,12 +322,12 @@
         in_specs=[vmem, hbm, vmem, vmem, hbm, hbm, hbm],
         out_specs=vmem,
         scratch_shapes=[
-            pltpu.VMEM((tok, expert_ids.shape[1]), jnp.int32),
+            pltpu.VMEM((expert_ids.shape[1], tok), jnp.int32),
             pltpu.VMEM((width, ff), bf),
             pltpu.VMEM((width, ff), bf),
             pltpu.VMEM((ff, width), bf),
-            pltpu.VMEM((128, tok), f32),
-            pltpu.VMEM((128, tok), f32),
+            pltpu.VMEM((NZ * NY, tok), f32),
+            pltpu.VMEM((NZ * NY, tok), f32),
             pltpu.VMEM((NZ, NY, 8, tok), f32),
             pltpu.VMEM((NZ, NY, 8, tok), f32),
             pltpu.VMEM((NZ, tok, width), bf),
@@ -348,25 +349,159 @@
         compiler_params=pltpu.CompilerParams(
             collective_id=0, has_side_effects=True, vmem_limit_bytes=60 * 2**20
         ),
-    )(tokens, expert_ids, gate_weights, span_ids, w_gate, w_up, w_down)
+    )(tokens, expert_ids.T, gate_weights.T, span_ids, w_gate, w_up, w_down)
+
+
+def at_x(d, e, dx):
+    return (lax.rem(d + 8 + 2 * dx, 8), e)
+
+
+def pack(g):
+    half = g.shape[0] // 2
+    tail = jnp.concatenate([g[:half, 256:], g[half:, 256:]], axis=1)
+    return jnp.concatenate([g[:, :128], g[:, 128:256], tail], axis=0)
+
+
+def unpack(p, rows):
+    half = rows // 2
+    tail = p[2 * rows :]
+    tail = jnp.concatenate([tail[:, :64], tail[:, 64:]], axis=0)
+    return jnp.concatenate([p[:rows], p[rows : 2 * rows], tail], axis=1)
+
+
+def project_kernel(
+    pooled, w_proj, cot, student, grad,
+    everyone, part, part_in, summed, summed_in,
+    x_ss, x_rs, s_ss, s_rs, y_ss, y_rs, z_ss, z_rs,
+):
+    d, z, y = place()
+    e = z * NY + y
+    x, core = d // 2, lax.rem(d, 2)
+    sibling = (2 * x + 1 - core, e)
+    spn, width = pooled.shape
+    rows = grad.shape[0]
+    band = NY * rows
+
+    barrier = pltpu.get_barrier_semaphore()
+    for dx in range(1, 4):
+        pl.semaphore_signal(barrier, inc=1, device_id=at_x(d, e, dx), device_id_type=MESH)
+    pl.semaphore_signal(barrier, inc=1, device_id=sibling, device_id_type=MESH)
+    for dz in DELTA[1:]:
+        pl.semaphore_signal(barrier, inc=1, device_id=at_z(d, z, y, dz), device_id_type=MESH)
+    for dy in range(1, NY):
+        pl.semaphore_signal(barrier, inc=1, device_id=at_y(d, z, y, dy), device_id_type=MESH)
+    everyone[d] = pooled[...]
+    pl.semaphore_wait(barrier, 3 + 1 + NZ - 1 + NY - 1)
+
+    def remote(src, dst, ss, rs, dev):
+        return pltpu.make_async_remote_copy(
+            src_ref=src, dst_ref=dst, send_sem=ss, recv_sem=rs, device_id=dev, device_id_type=MESH
+        )
+
+    started = []
+
+    def send(*what):
+        copy = remote(*what)
+        copy.start()
+        started.append(copy)
+
+    mine = everyone.at[d]
+    for dx in (1, 3, 2):
+        send(mine, mine, x_ss.at[dx], x_rs.at[4 - dx], at_x(d, e, dx))
+    send(mine, mine, s_ss.at[0], s_rs.at[0], sibling)
+    for dx in (1, 3, 2):
+        block = everyone.at[lax.rem(d + 2 * dx, 8)]
+        remote(block, block, x_ss.at[dx], x_rs.at[dx], (d, e)).wait_recv()
+        send(block, block, s_ss.at[dx], s_rs.at[dx], sibling)
+    for dx in (0, 1, 3, 2):
+        block = everyone.at[lax.rem(2 * (x + dx) + 1 - core, 8)]
+        remote(block, block, s_ss.at[dx], s_rs.at[dx], (d, e)).wait_recv()
+
+    groups = cot.shape[0]
+    order = (7, 5, 6, 3, 4, 1, 2, 0)
+    cot_all = cot[...].reshape(groups * spn, cot.shape[2])
+    for i in order:
+        there = lax.rem(z + NZ + DELTA[i], NZ)
+        at = pl.ds(pl.multiple_of(there * band, band), band)
+        lhs = everyone[:, :, at].reshape(groups * spn, band)
+        out = lax.dot_general(
+            lhs, cot_all, (((0,), (0,)), ((), ())), preferred_element_type=jnp.float32
+        ).astype(jnp.bfloat16)
+        for q in range(NY):
+            part[i, q] = pack(out[q * rows : (q + 1) * rows])
+        for j in range(1, NY):
+            send(
+                part.at[i, lax.rem(y + j, NY)], part_in.at[i, NY - j],
+                y_ss.at[i, j], y_rs.at[i, NY - j], at_y(d, z, y, j),
+            )
+
+    def body(n, carry):
+        g = 2 * n
+        out = lax.dot_general(
+            everyone[pl.ds(g, 2)].reshape(2 * spn, width), w_proj[...],
+            (((1,), (1,)), ((), ())), preferred_element_type=jnp.float32,
+        ).astype(jnp.bfloat16)
+        student[pl.ds(g, 2)] = out.reshape(2, spn, out.shape[1])
+        return carry
+
+    lax.fori_loop(0, groups // 2, body, 0)
+
+    for i in order:
+        for j in range(1, NY):
+            remote(
+                part.at[i, j], part_in.at[i, j], y_ss.at[i, j], y_rs.at[i, j], (d, e)
+            ).wait_recv()
+        total = part[i, y].astype(jnp.float32)
+        for j in range(1, NY):
+            total = total + part_in[i, j].astype(jnp.float32)
+        if i > 0:
+            summed[i] = total.astype(jnp.bfloat16)
+            send(
+                summed.at[i], summed_in.at[PAIR[i]], z_ss.at[i], z_rs.at[PAIR[i]],
+                at_z(d, z, y, DELTA[i]),
+            )
+    for i in order[:-1]:
+        remote(summed.at[i], summed_in.at[i], z_ss.at[i], z_rs.at[i], (d, e)).wait_recv()
+        total = total + summed_in[i].astype(jnp.float32)
+    grad[...] = unpack(total, rows)
+    for copy in started:
+        copy.wait_send()
+
+
+def project(pooled, w_proj, cotangent):
+    groups, spn, columns = cotangent.shape
+    width = pooled.shape[1]
+    rows = width // (NZ * NY)
+    vmem = pl.BlockSpec(memory_space=pltpu.VMEM)
+    bf = jnp.bfloat16
+    dma = pltpu.SemaphoreType.DMA
+    packed = (rows * columns // 128, 128)
+    return pl.pallas_call(
+        project_kernel,
+        out_shape=(
+            jax.ShapeDtypeStruct((groups, spn, columns), bf),
+            jax.ShapeDtypeStruct((rows, columns), jnp.float32),
+        ),
+        in_specs=[vmem] * 3,
+        out_specs=(vmem, vmem),
+        scratch_shapes=[
+            pltpu.VMEM((groups, spn, width), bf),
+            pltpu.VMEM((NZ, NY) + packed, bf),
+            pltpu.VMEM((NZ, NY) + packed, bf),
+            pltpu.VMEM((NZ,) + packed, bf),
+            pltpu.VMEM((NZ,) + packed, bf),
+            dma((4,)), dma((4,)), dma((4,)), dma((4,)),
+            dma((NZ, NY)), dma((NZ, NY)), dma((NZ,)), dma((NZ,)),
+        ],
+        compiler_params=pltpu.CompilerParams(
+            collective_id=1, has_side_effects=True, vmem_limit_bytes=60 * 2**20
+        ),
+    )(pooled, w_proj.T, cotangent)
 
 
 def local(tokens, expert_ids, gate_weights, span_ids, w_gate, w_up, w_down, w_proj, cotangent):
     pooled = moe(tokens, expert_ids, gate_weights, span_ids, w_gate, w_up, w_down)
-    pooled_all = lax.all_gather(pooled, "dp", axis=0, tiled=True)
-    columns = w_proj.shape[1]
-    student = jnp.dot(pooled_all, w_proj, preferred_element_type=jnp.float32).astype(jnp.bfloat16)
-    student = student.reshape(cotangent.shape)
-    cot_flat = cotangent.reshape(-1, columns)
-    grad_proj = lax.psum_scatter(
-        lax.dot_general(
-            pooled_all, cot_flat, (((0,), (0,)), ((), ())), preferred_element_type=jnp.float32
-        ),
-        "expert",
-        scatter_dimension=0,
-        tiled=True,
-    )
-    return (student, grad_proj)
+    return project(pooled, w_proj, cotangent)
 
 
 def solution(mesh):

time: 424 us -> 200 us (0.47)
  waiting for transfers between devices: 239 us -> 0 us
  Pallas kernels: 157 us -> 193 us
  between operations: 14.1 us -> 0.65 us
  matrix products: 6.14 us -> 0 us
    reduce_scatter x1 -> x0, waiting for transfers between devices: 216 us -> none  [local(): lax.psum_scatter(lax.dot_general(pooled_all, cot_flat, (((0,), (0,)), (()...]
    pallas_call x0 -> x1, Pallas kernels: none -> 36.3 us  [project(): pl.pallas_call(project_kernel, out_shape=(jax.ShapeDtypeStruct((groups, s...]
    all_gather x1 -> x0, waiting for transfers between devices: 23.3 us -> none  [local(): pooled_all = lax.all_gather(pooled, 'dp', axis=0, tiled=True)]
    dot_general x2 -> x0, matrix products: 6.14 us -> none  [the longest x1 4.53 us: local(): lax.dot_general(pooled_all, cot_flat, (((0,), (0,)), ((), ())), preferred...]
  transfers between devices with their start and end apart: 2 -> 0, of which waited for: 2 -> 0; matrix products, arithmetic and copies ran while one was open for 1% -> 0% of each run, Pallas kernels for 0% -> 0%
where the time goes in v2:
time: 200 us; the launch traced here: 197 us
  Pallas kernels  193 us (96%)
  local copies, waits for them, and re-layouts  3.32 us (2%)
    pallas_call x1, Pallas kernels, moe(): pl.pallas_call(moe_kernel, out_shape=jax.ShapeDtypeStruct((spn, width), b...  157 us
    pallas_call x1, Pallas kernels, project(): pl.pallas_call(project_kernel, out_shape=(jax.ShapeDtypeStruct((groups, s...  36.3 us

profile of v2, /device:TPU:2, one launch (start us, length us, event | category | flops | bytes accessed | tf_op | source)
XLA Modules:
  0.0 197.1 jit_solution(6618142583848650393)
XLA Ops:
  0.6 156.9 %shard_map.104.pooled = bf16[64,2048]{1,0:T(8,128)(2,1)} custom-call(bf16[128,2048]{1,0:T(8,128)(2,1)} %tokens.1, s32[8,4096]{1,0:T(8,128)} %bitcast.4, f32[8,128]{1,0:T(8,128)} %bitcast.5, s32[8,128]{1,0:T(8,128)} %spans.1, bf16[1,2048,768]{2,1,0:T(8,128)(2,1)} %wg_hbm.1, bf16[1,2048,768]{2,1,0:T(8,128)(2,1)} %wu_hbm.1, bf16[1,768,2048]{2,1,0:T(8,128)(2,1)} %wd_hbm.1), custom_call_target="tpu_custom_call" | custom-call | tf_op jit(solution)/shard_map/pallas_call | solution.py:319
  157.5 36.3 %shard_map.105 = (bf16[8,64,320]{2,1,0:T(8,128)(2,1)}, f32[64,320]{1,0:T(8,128)}) custom-call(bf16[64,2048]{1,0:T(8,128)(2,1)} %shard_map.104.pooled, bf16[320,2048]{1,0:T(8,128)(2,1)} %bitcast.3, bf16[8,64,320]{2,1,0:T(8,128)(2,1)} %cot.1), custom_call_target="tpu_custom_call" | custom-call | tf_op jit(solution)/shard_map/pallas_call | solution.py:479
  193.8 1.8 copy.13
  195.6 1.5 copy.14

commit v3 on v0

v3 whole, which is shorter than its diff:
```python
import jax
import jax.numpy as jnp
from jax import lax
from jax.experimental import pallas as pl
from jax.experimental.pallas import tpu as pltpu
from jax.sharding import PartitionSpec as P

MESH = pl.DeviceIdType.MESH
NX, NZ, NY = 4, 8, 4
CAP = 48
DELTA = (0, -1, 1, -2, 2, -3, 3, 4)
PAIR = (0, 2, 1, 4, 3, 6, 5, 7)
HOP = {4: (7, 7), 3: (6, 5), 2: (4, 3), 1: (2, 1)}
TILE = 256
WIDE = 512
ZA, YA, ZB, YB = 0, 1, 2, 3
COL = (0, 1024, 512, 1536)
OFF = (0, 0, 512, 512)
ON_Z = (True, False, True, False)
META, MY, Z, Y, B, CZ, CY, F, X, S, GY, GZ = range(12)


def place():
    d = lax.axis_index("dp")
    e = lax.axis_index("expert")
    return d, e // NY, lax.rem(e, NY)


def pack(g):
    half = g.shape[0] // 2
    tail = jnp.concatenate([g[:half, 256:], g[half:, 256:]], axis=1)
    return jnp.concatenate([g[:, :128], g[:, 128:256], tail], axis=0)


def unpack(p, rows):
    tail = p[2 * rows :]
    tail = jnp.concatenate([tail[:, :64], tail[:, 64:]], axis=0)
    return jnp.concatenate([p[:rows], p[rows : 2 * rows], tail], axis=1)


def kernel(
    tokens, ids_hbm, gates, spans, wg_hbm, wu_hbm, wd_hbm, proj_hbm, cot_hbm, student, grad,
    ids, wg, wu, wd, w_proj, cot, slot_t, gate_t, lines, meta_out, meta, meta_y, mix_y, mix_z,
    zbuf, sbuf, xbuf, hid, rbuf, bbuf, msg_y, got_y, msg_z, got_z, fin_out, fin_in,
    everyone, acc, part, part_in, summed, summed_in, own_sum,
    load_sem, send_sem, meta_rs, my_rs, z_rs, y_rs, b_rs, c_rs, f_rs, x_rs, s_rs, gy_rs, gz_rs,
):
    d, z, y = place()
    e = z * NY + y
    x, core = d // 2, lax.rem(d, 2)
    me = (d, e)
    sibling = (2 * x + 1 - core, e)
    tok, width = tokens.shape
    ff = wg.shape[1]
    groups, spn, columns = cot.shape
    rows = grad.shape[0]
    f32, bf = jnp.float32, jnp.bfloat16

    def at_z(dz):
        return (d, lax.rem(z + NZ + dz, NZ) * NY + y)

    def at_y(dy):
        return (d, z * NY + lax.rem(y + NY + dy, NY))

    def at_x(dx):
        return (lax.rem(d + 2 * NX + 2 * dx, 2 * NX), e)

    barrier = pltpu.get_barrier_semaphore()
    peers = [at_z(dz) for dz in DELTA[1:]]
    peers += [at_y(dy) for dy in range(1, NY)]
    peers += [at_x(dx) for dx in range(1, NX)] + [sibling]
    for peer in peers:
        pl.semaphore_signal(barrier, inc=1, device_id=peer, device_id_type=MESH)
    ids_copy = pltpu.make_async_copy(
        ids_hbm.at[:, pl.ds(pl.multiple_of(e * tok, tok), tok)], ids, load_sem.at[0]
    )
    ids_copy.start()
    loads = [
        pltpu.make_async_copy(src, dst, load_sem.at[n + 1])
        for n, (src, dst) in enumerate(
            (
                (wg_hbm.at[0], wg),
                (wu_hbm.at[0], wu),
                (wd_hbm.at[0], wd),
                (proj_hbm, w_proj),
                (cot_hbm, cot),
            )
        )
    ]
    for load in loads:
        load.start()
    def remote(src, dst, ss, rs, dev):
        return pltpu.make_async_remote_copy(
            src_ref=src, dst_ref=dst, send_sem=ss, recv_sem=rs, device_id=dev, device_id_type=MESH
        )

    def send(src, dst, kind, rs, dev):
        remote(src, dst, send_sem.at[kind], rs, dev).start()

    def sent(src, kind):
        remote(src, src, send_sem.at[kind], load_sem.at[0], me).wait_send()

    def arrive(dst, rs):
        remote(dst, dst, send_sem.at[0], rs, me).wait_recv()

    half = [pl.ds(h * (width // 2), width // 2) for h in (0, 1)]

    def z_send(src, s, h, dz):
        send(src.at[:, half[h]], zbuf.at[s, :, half[h]], Z, z_rs.at[s, h], at_z(dz))

    def z_recv(s, h):
        arrive(zbuf.at[s, :, half[h]], z_rs.at[s, h])

    ids_copy.wait()
    experts = NZ * NY
    number = lax.broadcasted_iota(jnp.int32, (experts, tok), 0)
    taken = jnp.zeros((experts, tok), f32)
    weight = jnp.zeros((experts, tok), f32)
    for k in range(ids.shape[0]):
        named = ids[k : k + 1, :] == number
        taken = taken + jnp.where(named, 1.0, 0.0)
        weight = weight + jnp.where(named, gates[k : k + 1, :], 0.0)
    row = lax.broadcasted_iota(jnp.int32, (tok, tok), 0)
    col = lax.broadcasted_iota(jnp.int32, (tok, tok), 1)
    earlier = jnp.where(row < col, 1.0, 0.0).astype(bf)
    before = jnp.dot(taken.astype(bf), earlier, preferred_element_type=f32)
    slot_t[...] = jnp.where(taken > 0.0, before, -1.0)
    gate_t[...] = weight
    own_span = spans[pl.ds(d, 1), :].astype(f32)
    lines[...] = jnp.zeros(lines.shape, f32)
    for i in range(NZ):
        there = lax.rem(z + NZ + DELTA[i], NZ) * NY
        for j in range(NY):
            line = there + lax.rem(y + j, NY)
            lines[i, j : j + 1, :] = slot_t[pl.ds(line, 1), :]
            lines[i, NY + j : NY + j + 1, :] = gate_t[pl.ds(line, 1), :]
        lines[i, 2 * NY : 2 * NY + 1, :] = own_span
        if i == 0:
            meta[0] = lines[0].astype(bf)
        else:
            meta_out[i] = lines[i].astype(bf)
    pl.semaphore_wait(barrier, len(peers))
    for i in range(1, NZ):
        send(meta_out.at[i], meta.at[PAIR[i]], META, meta_rs.at[0], at_z(DELTA[i]))
    for h in (0, 1):
        z_send(tokens, 1, h, 1)
        z_send(tokens, 2, h, -1)

    slots = lax.broadcasted_iota(jnp.int32, (CAP, tok), 0).astype(f32)
    span_rows = lax.broadcasted_iota(jnp.int32, (spn, tok), 0).astype(f32)
    last = (((1,), (1,)), ((), ()))

    def onehot(slab, j):
        return jnp.where(slab[j : j + 1, :] == slots, 1.0, 0.0).astype(bf)

    def dispatch(i, h):
        block = tokens if i == 0 else zbuf.at[i]
        slab = meta[i].astype(f32)
        pick = jnp.concatenate([onehot(slab, j) for j in range(NY)], axis=0)

        def body(n, carry):
            at = pl.ds(pl.multiple_of(h * (width // 2) + n * 512, 512), 512)
            out = jnp.dot(pick, block[:, at], preferred_element_type=f32).astype(bf)
            xbuf[i, 0:CAP, at] = out[0:CAP]
            sbuf[i, :, at] = out[CAP:]
            return carry

        lax.fori_loop(0, width // 1024, body, 0)
        for j in range(1, NY):
            back = NY - j
            send(
                sbuf.at[i, pl.ds((j - 1) * CAP, CAP), half[h]],
                xbuf.at[i, pl.ds(back * CAP, CAP), half[h]],
                Y, y_rs.at[i], at_y(j),
            )

    def ffn(i):
        arrive(xbuf.at[i, pl.ds(CAP, (NY - 1) * CAP)], y_rs.at[i])

        def up(n, carry):
            at = pl.ds(pl.multiple_of(n * TILE, TILE), TILE)
            rows_in = xbuf[i]
            g = jnp.dot(rows_in, wg[:, at], preferred_element_type=f32)
            u = jnp.dot(rows_in, wu[:, at], preferred_element_type=f32)
            hid[:, at] = (g / (1.0 + jnp.exp(-g)) * u).astype(bf)
            return carry

        lax.fori_loop(0, ff // TILE, up, 0)
        for c in range(4):

            def down(n, carry):
                at = pl.ds(pl.multiple_of(COL[c] + n * TILE, TILE), TILE)
                out = jnp.dot(hid[...], wd[:, at], preferred_element_type=f32).astype(bf)
                rbuf[i, :, at] = out
                if not ON_Z[c]:
                    own = pl.ds(pl.multiple_of(OFF[c] + n * TILE, TILE), TILE)
                    bbuf[i, 0:CAP, own] = out[0:CAP]
                return carry

            lax.fori_loop(0, WIDE // TILE, down, 0)

    def pooling(slab, j):
        gate = slab[NY + j : NY + j + 1, :]
        share = jnp.where(slab[2 * NY : 2 * NY + 1, :] == span_rows, gate, 0.0).astype(bf)
        out = lax.dot_general(share, onehot(slab, j), last, preferred_element_type=f32)
        return out.astype(bf)

    def mixing(i):
        own = meta[i].astype(f32)
        mix_y[i] = jnp.concatenate([pooling(own, j) for j in range(NY)], axis=1)
        for j in range(NY):
            slab = own if j == 0 else meta_y[j, i].astype(f32)
            mine = pooling(slab, (NY - j) % NY)
            pieces = [mine if q == j else jnp.zeros((spn, CAP), bf) for q in range(NY)]
            mix_z[i, j * spn : (j + 1) * spn] = jnp.concatenate(pieces, axis=1)

    def give_back(c, i):
        src = pl.ds(COL[c], WIDE)
        dst = pl.ds(OFF[c], WIDE)
        for j in range(1, NY):
            back = NY - j
            send(
                rbuf.at[i, pl.ds(j * CAP, CAP), src], bbuf.at[i, pl.ds(back * CAP, CAP), dst],
                B, b_rs.at[c // 2, i], at_y(j),
            )

    def returned(c, i):
        arrive(
            bbuf.at[i, pl.ds(CAP, (NY - 1) * CAP), pl.ds(OFF[c], WIDE)], b_rs.at[c // 2, i]
        )

    def term(c, i, n, part_rows=None):
        mix = mix_z.at[i] if ON_Z[c] else mix_y.at[i]
        mix = mix[...] if part_rows is None else mix[part_rows, :]
        if ON_Z[c]:
            block = rbuf[i, :, pl.ds(COL[c] + n * TILE, TILE)]
        else:
            block = bbuf[i, :, pl.ds(OFF[c] + n * TILE, TILE)]
        return jnp.dot(mix, block, preferred_element_type=f32)

    def chain_part(buf, c, way, hop):
        at = pl.ds(OFF[c], WIDE)
        total = buf.shape[2]
        if hop == NZ // 2:
            return buf.at[way, hop - 1, pl.ds(way * (total // 2), total // 2), at]
        return buf.at[way, hop - 1, :, at]

    def chain_recv(c, way, hop):
        got = got_z if ON_Z[c] else got_y
        arrive(chain_part(got, c, way, hop), c_rs.at[c, way, hop - 1])

    def pass_on(c, hop):
        msg, got = (msg_z, got_z) if ON_Z[c] else (msg_y, got_y)
        half = msg.shape[2] // 2
        for way in (0, 1):
            i = HOP[hop][way]
            if not ON_Z[c] and not (hop == 4 and way == 1):
                returned(c, i)
            if hop < 4:
                chain_recv(c, way, hop + 1)
            side, other = pl.ds(way * half, half), pl.ds((1 - way) * half, half)
            for n in range(WIDE // TILE):
                at = pl.ds(OFF[c] + n * TILE, TILE)
                if hop == 4:
                    msg[way, 3, side, at] = term(c, i, n, side).astype(bf)
                elif hop == 3:
                    came = got[way, 3, side, at].astype(f32)
                    msg[way, 2, side, at] = (term(c, i, n, side) + came).astype(bf)
                    msg[way, 2, other, at] = term(c, i, n, other).astype(bf)
                else:
                    came = got[way, hop, :, at].astype(f32)
                    msg[way, hop - 1, :, at] = (term(c, i, n) + came).astype(bf)
            send(
                chain_part(msg, c, way, hop), chain_part(got, c, way, hop),
                CZ if ON_Z[c] else CY, c_rs.at[c, way, hop - 1], at_z(1 - 2 * way),
            )

    count = jnp.sum(jnp.where(own_span == span_rows, 1.0, 0.0), axis=1, keepdims=True)

    def spread(c):
        mine = everyone.at[d, :, pl.ds(COL[c], WIDE)]
        for dx in (1, 3, 2):
            send(mine, mine, X, x_rs.at[c], at_x(dx))
        send(mine, mine, S, s_rs.at[c], sibling)

    def finish_z(c):
        chain_recv(c, 0, 1)
        chain_recv(c, 1, 1)
        for n in range(WIDE // TILE):
            at = pl.ds(OFF[c] + n * TILE, TILE)
            total = term(c, 0, n) + got_z[0, 0, :, at].astype(f32) + got_z[1, 0, :, at].astype(f32)
            fin_out[:, :, at] = total.astype(bf).reshape(NY, spn, TILE)
        at = pl.ds(OFF[c], WIDE)
        for j in range(1, NY):
            send(
                fin_out.at[j, :, at], fin_in.at[NY - j, :, at],
                F, f_rs.at[c // 2], at_y(j),
            )

    def finish_z_pooled(c):
        at = pl.ds(OFF[c], WIDE)
        total = fin_out[0, :, at].astype(f32)
        arrive(fin_in.at[pl.ds(1, NY - 1), :, at], f_rs.at[c // 2])
        for j in range(1, NY):
            total = total + fin_in[j, :, at].astype(f32)
        everyone[d, :, pl.ds(COL[c], WIDE)] = (total / count).astype(bf)
        spread(c)

    def finish_y(c):
        returned(c, 0)
        chain_recv(c, 0, 1)
        chain_recv(c, 1, 1)
        for n in range(WIDE // TILE):
            at = pl.ds(OFF[c] + n * TILE, TILE)
            total = term(c, 0, n) + got_y[0, 0, :, at].astype(f32) + got_y[1, 0, :, at].astype(f32)
            everyone[d, :, pl.ds(COL[c] + n * TILE, TILE)] = (total / count).astype(bf)
        spread(c)

    def relay(c):
        at = pl.ds(COL[c], WIDE)
        arrive(everyone.at[pl.ds(0, NX - 1), :, at], x_rs.at[c])
        for dx in (1, 3, 2):
            block = everyone.at[lax.rem(d + 2 * dx, 2 * NX), :, at]
            send(block, block, S, s_rs.at[c], sibling)

    def gathered(c):
        arrive(everyone.at[pl.ds(0, NX), :, pl.ds(COL[c], WIDE)], s_rs.at[c])

    band = NY * rows

    def bands(c):
        return range(COL[c] // band, (COL[c] + WIDE) // band)

    def gradient(c):
        cot_all = cot[...].reshape(groups * spn, columns)
        for b in bands(c):
            lhs = everyone[:, :, pl.ds(b * band, band)].reshape(groups * spn, band)
            out = lax.dot_general(
                lhs, cot_all, (((0,), (0,)), ((), ())), preferred_element_type=f32
            ).astype(bf)
            for q in range(NY):
                part[b, q] = pack(out[q * rows : (q + 1) * rows])
            for j in range(1, NY):
                send(
                    part.at[b, lax.rem(y + j, NY)], part_in.at[b, NY - j],
                    GY, gy_rs.at[b], at_y(j),
                )

    def to_owner(b):
        send(summed.at[b], summed_in.at[z], GZ, gz_rs.at[0], (d, b * NY + y))

    def gather_band(b):
        arrive(part_in.at[b, pl.ds(1, NY - 1)], gy_rs.at[b])
        total = part[b, y].astype(f32)
        for j in range(1, NY):
            total = total + part_in[b, j].astype(f32)

        @pl.when(z == b)
        def _():
            own_sum[...] = total

        @pl.when(z != b)
        def _():
            summed[b] = total.astype(bf)
            to_owner(b)

    def project(c, first=False, final=False):
        def body(n, carry):
            g = pl.ds(2 * n, 2)
            out = lax.dot_general(
                everyone[g, :, pl.ds(COL[c], WIDE)].reshape(2 * spn, WIDE),
                w_proj[:, pl.ds(COL[c], WIDE)], last, preferred_element_type=f32,
            ).reshape(2, spn, columns)
            if not first:
                out = out + acc[g]
            if final:
                student[g] = out.astype(bf)
            else:
                acc[g] = out
            return carry

        lax.fori_loop(0, groups // 2, body, 0)

    for h in (0, 1):
        dispatch(0, h)
    arrive(meta.at[pl.ds(1, NZ - 1)], meta_rs.at[0])
    for p in (1, 2, 3):
        a, b = 2 * p - 1, 2 * p
        for h in (0, 1):
            z_recv(a, h)
            if p < 3:
                z_send(zbuf.at[a], a + 2, h, 1)
            elif h == 0:
                z_send(zbuf.at[a], 7, h, 1)
            z_recv(b, h)
            if p < 3:
                z_send(zbuf.at[b], b + 2, h, -1)
            elif h == 1:
                z_send(zbuf.at[b], 7, h, -1)
            dispatch(a, h)
            if p == 1:
                dispatch(b, h)
        if p == 1:
            for j in range(1, NY):
                send(meta, meta_y.at[NY - j], MY, my_rs.at[0], at_y(j))
            for load in loads:
                load.wait()
            ffn(0)
        if p == 2:
            ffn(1)
        if p == 3:
            ffn(2)
    for h in (0, 1):
        z_recv(7, h)
        dispatch(7, h)
    for i in (6, 4):
        for h in (0, 1):
            dispatch(i, h)
    arrive(meta_y.at[pl.ds(1, NY - 1)], my_rs.at[0])
    for i in range(NZ):
        mixing(i)
    for i in (3, 5, 7):
        ffn(i)
    pass_on(ZA, 4)
    pass_on(ZB, 4)
    ffn(6)
    for i in (5, 7, 6):
        give_back(YA, i)
    pass_on(ZA, 3)
    pass_on(ZB, 3)
    ffn(4)
    give_back(YA, 3)
    give_back(YA, 4)
    pass_on(ZA, 2)
    for i in (1, 2, 0):
        give_back(YA, i)
    pass_on(YA, 4)
    pass_on(ZB, 2)
    pass_on(YA, 3)
    pass_on(ZA, 1)
    for i in (5, 7, 6):
        give_back(YB, i)
    pass_on(YA, 2)
    pass_on(ZB, 1)
    pass_on(YA, 1)
    finish_z(ZA)
    for i in (3, 4, 1, 2, 0):
        give_back(YB, i)
    finish_y(YA)
    pass_on(YB, 4)
    pass_on(YB, 3)
    finish_z_pooled(ZA)
    finish_z(ZB)
    pass_on(YB, 2)
    relay(YA)
    relay(ZA)
    pass_on(YB, 1)
    gathered(YA)
    gradient(YA)
    finish_z_pooled(ZB)
    gathered(ZA)
    gradient(ZA)
    finish_y(YB)
    project(YA, first=True)
    project(ZA)
    for b in list(bands(YA)) + list(bands(ZA)):
        gather_band(b)
    relay(ZB)
    relay(YB)
    gathered(ZB)
    gradient(ZB)
    gathered(YB)
    gradient(YB)
    project(ZB)
    project(YB, final=True)
    for b in list(bands(ZB)) + list(bands(YB)):
        gather_band(b)
    arrive(summed_in.at[pl.ds(0, NZ - 1)], gz_rs.at[0])
    total = own_sum[...]
    for dz in range(1, NZ):
        src = lax.rem(z + dz, NZ)
        total = total + summed_in[src].astype(f32)
    grad[...] = unpack(total, rows)
    sent(meta_out.at[pl.ds(1, NZ - 1)], META)
    sent(meta_y.at[pl.ds(1, NY - 1)], MY)
    sent(zbuf.at[pl.ds(1, NZ - 1)], Z)
    sent(sbuf, Y)
    sent(bbuf.at[:, pl.ds(CAP, (NY - 1) * CAP)], B)
    for kind, buf in ((CZ, msg_z), (CY, msg_y)):
        sent(buf.at[:, :, :, pl.ds(0, 7 * buf.shape[3] // 8)], kind)
    sent(fin_out.at[pl.ds(1, NY - 1)], F)
    sent(everyone.at[pl.ds(0, NX - 1)], X)
    sent(everyone.at[pl.ds(0, NX)], S)
    sent(part.at[:, pl.ds(1, NY - 1)], GY)
    sent(summed.at[pl.ds(1, NZ - 1)], GZ)


def hand_on(student_in, grad_in, student, grad):
    student[...] = student_in[...]
    grad[...] = grad_in[...]


def local(tokens, expert_ids, gate_weights, span_ids, w_gate, w_up, w_down, w_proj, cotangent):
    tok, width = tokens.shape
    ff = w_gate.shape[2]
    topk = expert_ids.shape[1]
    spn = tok // 2
    groups, _, columns = cotangent.shape
    rows = width // (NZ * NY)
    packed = (rows * columns // 128, 128)
    bf, f32 = jnp.bfloat16, jnp.float32
    vmem = pl.BlockSpec(memory_space=pltpu.VMEM)
    hbm = pl.BlockSpec(memory_space=pl.ANY)
    scratch, dma = pltpu.VMEM, pltpu.SemaphoreType.DMA
    results = pl.pallas_call(
        kernel,
        out_shape=(
            jax.ShapeDtypeStruct((groups, spn, columns), bf),
            jax.ShapeDtypeStruct((rows, columns), f32),
        ),
        in_specs=[vmem, hbm, vmem, vmem, hbm, hbm, hbm, hbm, hbm],
        out_specs=(vmem, vmem),
        scratch_shapes=[
            scratch((topk, tok), jnp.int32),
            scratch((width, ff), bf),
            scratch((width, ff), bf),
            scratch((ff, width), bf),
            scratch((columns, width), bf),
            scratch((groups, spn, columns), bf),
            scratch((NZ * NY, tok), f32),
            scratch((NZ * NY, tok), f32),
            scratch((NZ, 16, tok), f32),
            scratch((NZ, 16, tok), bf),
            scratch((NZ, 16, tok), bf),
            scratch((NY, NZ, 16, tok), bf),
            scratch((NZ, spn, NY * CAP), bf),
            scratch((NZ, NY * spn, NY * CAP), bf),
            scratch((NZ, tok, width), bf),
            scratch((NZ, (NY - 1) * CAP, width), bf),
            scratch((NZ, NY * CAP, width), bf),
            scratch((NY * CAP, ff), bf),
            scratch((NZ, NY * CAP, width), bf),
            scratch((NZ, NY * CAP, 2 * WIDE), bf),
            scratch((2, NZ // 2, spn, 2 * WIDE), bf),
            scratch((2, NZ // 2, spn, 2 * WIDE), bf),
            scratch((2, NZ // 2, NY * spn, 2 * WIDE), bf),
            scratch((2, NZ // 2, NY * spn, 2 * WIDE), bf),
            scratch((NY, spn, 2 * WIDE), bf),
            scratch((NY, spn, 2 * WIDE), bf),
            scratch((groups, spn, width), bf),
            scratch((groups, spn, columns), f32),
            scratch((NZ, NY) + packed, bf),
            scratch((NZ, NY) + packed, bf),
            scratch((NZ,) + packed, bf),
            scratch((NZ,) + packed, bf),
            scratch(packed, f32),
            dma((6,)),
            dma((12,)),
            dma((1,)),
            dma((1,)),
            dma((NZ, 2)),
            dma((NZ,)),
            dma((2, NZ)),
            dma((4, 2, NZ // 2)),
            dma((2,)),
            dma((4,)),
            dma((4,)),
            dma((NZ,)),
            dma((1,)),
        ],
        compiler_params=pltpu.CompilerParams(
            collective_id=0, has_side_effects=True, vmem_limit_bytes=62 * 2**20
        ),
    )(
        tokens, expert_ids.T, gate_weights.T, span_ids, w_gate, w_up, w_down, w_proj.T, cotangent
    )
    return pl.pallas_call(
        hand_on,
        out_shape=[jax.ShapeDtypeStruct(r.shape, r.dtype) for r in results],
        in_specs=[vmem] * 2,
        out_specs=[vmem] * 2,
    )(*results)


def solution(mesh):
    placed = (
        P(("dp", "expert"), None),
        P("dp", None),
        P(("dp", "expert"), None),
        P(None, "expert"),
        P("expert", None, None),
        P("expert", None, None),
        P("expert", None, None),
        P(None, "dp"),
        P(None, "expert", "dp"),
    )
    return jax.shard_map(
        local,
        mesh=mesh,
        in_specs=placed,
        out_specs=(P(None, "expert", "dp"), P("expert", "dp")),
        check_vma=False,
    )
```

time: 647 us -> 156 us (0.24)
  waiting for transfers between devices: 385 us -> 0 us
  local copies, waits for them, and re-layouts: 189 us -> 0 us
  Pallas kernels: 0 us -> 155 us
  matrix products: 30.2 us -> 0 us
  other arithmetic: 15.6 us -> 0 us
  between operations: 14 us -> 0.64 us
  starting transfers between devices: 11.9 us -> 0 us
    reduce_scatter x1 -> x0, waiting for transfers between devices: 217 us -> none  [local(): lax.psum_scatter(lax.dot_general(pooled_all, cot_flat, (((0,), (0,)), (()...]
    pallas_call x0 -> x2, Pallas kernels: none -> 155 us  [the longest x1 153 us: local(): pl.pallas_call(kernel, out_shape=(jax.ShapeDtypeStruct((groups, spn, colu...]
    all_to_all x1 -> x0, waiting for transfers between devices: 138 us -> none  [local(): lax.all_to_all(result, 'expert', split_axis=0, concat_axis=0, tiled=True)]
    unnamed x33 -> x0, local copies, waits for them, and re-layouts: 126 us -> none
    gather x2 -> x0, local copies, waits for them, and re-layouts: 33 us -> none  [the longest x1 20.7 us: local(): arrived = jnp.take(padded, index, axis=0)]
    dot_general x7 -> x0, matrix products: 30.2 us -> none  [the longest x1 7.26 us: local(): jnp.dot(hidden, w_down[0], preferred_element_type=jnp.float32)]
    all_gather x2 -> x0, waiting for transfers between devices: 29.4 us -> none  [the longest x1 29.4 us: local(): pooled_all = lax.all_gather(pooled, 'dp', axis=0, tiled=True)]
    concatenate x1 -> x0, local copies, waits for them, and re-layouts: 13.9 us -> none  [local(): padded = jnp.concatenate([everyone, zero_row], axis=0)]
  transfers between devices with their start and end apart: 4 -> 0, of which waited for: 3 -> 0; matrix products, arithmetic and copies ran while one was open for 24% -> 0% of each run, Pallas kernels for 0% -> 0%
where the time goes in v3:
time: 156 us
  Pallas kernels  155 us (99%)
    pallas_call x1, Pallas kernels, local(): pl.pallas_call(kernel, out_shape=(jax.ShapeDtypeStruct((groups, spn, colu...  153 us

profile of v3, /device:TPU:2, one launch (start us, length us, event | category | flops | bytes accessed | tf_op | source)
XLA Modules:
  0.0 155.8 jit_solution(1686323015356395067)
XLA Ops:
  0.6 153.4 %shard_map.104 = (bf16[8,64,320]{2,1,0:T(8,128)(2,1)}, f32[64,320]{1,0:T(8,128)}) custom-call(bf16[128,2048]{1,0:T(8,128)(2,1)} %tokens.1, s32[8,4096]{1,0:T(8,128)} %bitcast.4, f32[8,128]{1,0:T(8,128)} %bitcast.5, s32[8,128]{1,0:T(8,128)} %spans.1, bf16[1,2048,768]{2,1,0:T(8,128)(2,1)} %wg_hbm.1, bf16[1,2048,768]{2,1,0:T(8,128)(2,1)} %wu_hbm.1, ...), custom_call_target="tpu_custom_call" | custom-call | tf_op jit(solution)/shard_map/pallas_call | solution.py:515
  154.0 1.8 %shard_map.105 = (bf16[8,64,320]{2,1,0:T(8,128)(2,1)}, f32[64,320]{1,0:T(8,128)}) custom-call(bf16[8,64,320]{2,1,0:T(8,128)(2,1)} %get-tuple-element.4.student_in, f32[64,320]{1,0:T(8,128)} %get-tuple-element.5.grad_in), custom_call_target="tpu_custom_call" | custom-call | tf_op jit(solution)/shard_map/pallas_call | solution.py:577

commit v4 on v3

--- a/solution.py
+++ b/solution.py
@@ -12,11 +12,13 @@
 PAIR = (0, 2, 1, 4, 3, 6, 5, 7)
 HOP = {4: (7, 7), 3: (6, 5), 2: (4, 3), 1: (2, 1)}
 TILE = 256
-WIDE = 512
 ZA, YA, ZB, YB = 0, 1, 2, 3
-COL = (0, 1024, 512, 1536)
-OFF = (0, 0, 512, 512)
 ON_Z = (True, False, True, False)
+WIDE = (512, 512, 512, 512)
+COL = (0, WIDE[0], WIDE[0] + WIDE[1], sum(WIDE[:3]))
+OFF = (0, 0, WIDE[0], WIDE[1])
+Z_WIDE, Y_WIDE = WIDE[0] + WIDE[2], WIDE[1] + WIDE[3]
+BAND = (0, 4, 2, 6, 1, 5, 3, 7)
 META, MY, Z, Y, B, CZ, CY, F, X, S, GY, GZ = range(12)
 
 
@@ -81,14 +83,21 @@
             (
                 (wg_hbm.at[0], wg),
                 (wu_hbm.at[0], wu),
+                (cot_hbm, cot),
                 (wd_hbm.at[0], wd),
                 (proj_hbm, w_proj),
-                (cot_hbm, cot),
             )
         )
     ]
-    for load in loads:
+    for load in loads[:3]:
         load.start()
+    wide_band = width // NZ
+    for n, (src, dst) in ((4, (wd_hbm.at[0], wd)), (5, (proj_hbm, w_proj))):
+        for p in range(NZ):
+            there = pl.ds(BAND[p] * wide_band, wide_band)
+            here = pl.ds(p * wide_band, wide_band)
+            pltpu.make_async_copy(src.at[:, there], dst.at[:, here], load_sem.at[n]).start()
+
     def remote(src, dst, ss, rs, dev):
         return pltpu.make_async_remote_copy(
             src_ref=src, dst_ref=dst, send_sem=ss, recv_sem=rs, device_id=dev, device_id_type=MESH
@@ -139,13 +148,6 @@
             meta[0] = lines[0].astype(bf)
         else:
             meta_out[i] = lines[i].astype(bf)
-    pl.semaphore_wait(barrier, len(peers))
-    for i in range(1, NZ):
-        send(meta_out.at[i], meta.at[PAIR[i]], META, meta_rs.at[0], at_z(DELTA[i]))
-    for h in (0, 1):
-        z_send(tokens, 1, h, 1)
-        z_send(tokens, 2, h, -1)
-
     slots = lax.broadcasted_iota(jnp.int32, (CAP, tok), 0).astype(f32)
     span_rows = lax.broadcasted_iota(jnp.int32, (spn, tok), 0).astype(f32)
     last = (((1,), (1,)), ((), ()))
@@ -153,7 +155,7 @@
     def onehot(slab, j):
         return jnp.where(slab[j : j + 1, :] == slots, 1.0, 0.0).astype(bf)
 
-    def dispatch(i, h):
+    def select(i, h):
         block = tokens if i == 0 else zbuf.at[i]
         slab = meta[i].astype(f32)
         pick = jnp.concatenate([onehot(slab, j) for j in range(NY)], axis=0)
@@ -166,6 +168,10 @@
             return carry
 
         lax.fori_loop(0, width // 1024, body, 0)
+
+    def dispatch(i, h):
+        if i > 0:
+            select(i, h)
         for j in range(1, NY):
             back = NY - j
             send(
@@ -197,7 +203,7 @@
                     bbuf[i, 0:CAP, own] = out[0:CAP]
                 return carry
 
-            lax.fori_loop(0, WIDE // TILE, down, 0)
+            lax.fori_loop(0, WIDE[c] // TILE, down, 0)
 
     def pooling(slab, j):
         gate = slab[NY + j : NY + j + 1, :]
@@ -215,8 +221,8 @@
             mix_z[i, j * spn : (j + 1) * spn] = jnp.concatenate(pieces, axis=1)
 
     def give_back(c, i):
-        src = pl.ds(COL[c], WIDE)
-        dst = pl.ds(OFF[c], WIDE)
+        src = pl.ds(COL[c], WIDE[c])
+        dst = pl.ds(OFF[c], WIDE[c])
         for j in range(1, NY):
             back = NY - j
             send(
@@ -226,7 +232,7 @@
 
     def returned(c, i):
         arrive(
-            bbuf.at[i, pl.ds(CAP, (NY - 1) * CAP), pl.ds(OFF[c], WIDE)], b_rs.at[c // 2, i]
+            bbuf.at[i, pl.ds(CAP, (NY - 1) * CAP), pl.ds(OFF[c], WIDE[c])], b_rs.at[c // 2, i]
         )
 
     def term(c, i, n, part_rows=None):
@@ -239,7 +245,7 @@
         return jnp.dot(mix, block, preferred_element_type=f32)
 
     def chain_part(buf, c, way, hop):
-        at = pl.ds(OFF[c], WIDE)
+        at = pl.ds(OFF[c], WIDE[c])
         total = buf.shape[2]
         if hop == NZ // 2:
             return buf.at[way, hop - 1, pl.ds(way * (total // 2), total // 2), at]
@@ -259,7 +265,7 @@
             if hop < 4:
                 chain_recv(c, way, hop + 1)
             side, other = pl.ds(way * half, half), pl.ds((1 - way) * half, half)
-            for n in range(WIDE // TILE):
+            for n in range(WIDE[c] // TILE):
                 at = pl.ds(OFF[c] + n * TILE, TILE)
                 if hop == 4:
                     msg[way, 3, side, at] = term(c, i, n, side).astype(bf)
@@ -278,7 +284,7 @@
     count = jnp.sum(jnp.where(own_span == span_rows, 1.0, 0.0), axis=1, keepdims=True)
 
     def spread(c):
-        mine = everyone.at[d, :, pl.ds(COL[c], WIDE)]
+        mine = everyone.at[d, :, pl.ds(COL[c], WIDE[c])]
         for dx in (1, 3, 2):
             send(mine, mine, X, x_rs.at[c], at_x(dx))
         send(mine, mine, S, s_rs.at[c], sibling)
@@ -286,11 +292,11 @@
     def finish_z(c):
         chain_recv(c, 0, 1)
         chain_recv(c, 1, 1)
-        for n in range(WIDE // TILE):
+        for n in range(WIDE[c] // TILE):
             at = pl.ds(OFF[c] + n * TILE, TILE)
             total = term(c, 0, n) + got_z[0, 0, :, at].astype(f32) + got_z[1, 0, :, at].astype(f32)
             fin_out[:, :, at] = total.astype(bf).reshape(NY, spn, TILE)
-        at = pl.ds(OFF[c], WIDE)
+        at = pl.ds(OFF[c], WIDE[c])
         for j in range(1, NY):
             send(
                 fin_out.at[j, :, at], fin_in.at[NY - j, :, at],
@@ -298,43 +304,47 @@
             )
 
     def finish_z_pooled(c):
-        at = pl.ds(OFF[c], WIDE)
+        at = pl.ds(OFF[c], WIDE[c])
         total = fin_out[0, :, at].astype(f32)
         arrive(fin_in.at[pl.ds(1, NY - 1), :, at], f_rs.at[c // 2])
         for j in range(1, NY):
             total = total + fin_in[j, :, at].astype(f32)
-        everyone[d, :, pl.ds(COL[c], WIDE)] = (total / count).astype(bf)
+        everyone[d, :, pl.ds(COL[c], WIDE[c])] = (total / count).astype(bf)
         spread(c)
 
     def finish_y(c):
         returned(c, 0)
         chain_recv(c, 0, 1)
         chain_recv(c, 1, 1)
-        for n in range(WIDE // TILE):
+        for n in range(WIDE[c] // TILE):
             at = pl.ds(OFF[c] + n * TILE, TILE)
             total = term(c, 0, n) + got_y[0, 0, :, at].astype(f32) + got_y[1, 0, :, at].astype(f32)
             everyone[d, :, pl.ds(COL[c] + n * TILE, TILE)] = (total / count).astype(bf)
         spread(c)
 
     def relay(c):
-        at = pl.ds(COL[c], WIDE)
+        at = pl.ds(COL[c], WIDE[c])
         arrive(everyone.at[pl.ds(0, NX - 1), :, at], x_rs.at[c])
         for dx in (1, 3, 2):
             block = everyone.at[lax.rem(d + 2 * dx, 2 * NX), :, at]
             send(block, block, S, s_rs.at[c], sibling)
 
     def gathered(c):
-        arrive(everyone.at[pl.ds(0, NX), :, pl.ds(COL[c], WIDE)], s_rs.at[c])
+        arrive(everyone.at[pl.ds(0, NX), :, pl.ds(COL[c], WIDE[c])], s_rs.at[c])
 
     band = NY * rows
 
+    def places(c):
+        return range(COL[c] // band, (COL[c] + WIDE[c]) // band)
+
     def bands(c):
-        return range(COL[c] // band, (COL[c] + WIDE) // band)
+        return [BAND[p] for p in places(c)]
 
     def gradient(c):
         cot_all = cot[...].reshape(groups * spn, columns)
-        for b in bands(c):
-            lhs = everyone[:, :, pl.ds(b * band, band)].reshape(groups * spn, band)
+        for p in places(c):
+            b = BAND[p]
+            lhs = everyone[:, :, pl.ds(p * band, band)].reshape(groups * spn, band)
             out = lax.dot_general(
                 lhs, cot_all, (((0,), (0,)), ((), ())), preferred_element_type=f32
             ).astype(bf)
@@ -368,8 +378,8 @@
         def body(n, carry):
             g = pl.ds(2 * n, 2)
             out = lax.dot_general(
-                everyone[g, :, pl.ds(COL[c], WIDE)].reshape(2 * spn, WIDE),
-                w_proj[:, pl.ds(COL[c], WIDE)], last, preferred_element_type=f32,
+                everyone[g, :, pl.ds(COL[c], WIDE[c])].reshape(2 * spn, WIDE[c]),
+                w_proj[:, pl.ds(COL[c], WIDE[c])], last, preferred_element_type=f32,
             ).reshape(2, spn, columns)
             if not first:
                 out = out + acc[g]
@@ -381,6 +391,14 @@
 
         lax.fori_loop(0, groups // 2, body, 0)
 
+    for h in (0, 1):
+        select(0, h)
+    pl.semaphore_wait(barrier, len(peers))
+    for i in range(1, NZ):
+        send(meta_out.at[i], meta.at[PAIR[i]], META, meta_rs.at[0], at_z(DELTA[i]))
+    for h in (0, 1):
+        z_send(tokens, 1, h, 1)
+        z_send(tokens, 2, h, -1)
     for h in (0, 1):
         dispatch(0, h)
     arrive(meta.at[pl.ds(1, NZ - 1)], meta_rs.at[0])
@@ -424,28 +442,34 @@
     pass_on(ZA, 4)
     pass_on(ZB, 4)
     ffn(6)
-    for i in (5, 7, 6):
-        give_back(YA, i)
+    give_back(YA, 5)
+    give_back(YA, 7)
+    give_back(YA, 6)
     pass_on(ZA, 3)
     pass_on(ZB, 3)
     ffn(4)
     give_back(YA, 3)
     give_back(YA, 4)
     pass_on(ZA, 2)
-    for i in (1, 2, 0):
-        give_back(YA, i)
+    give_back(YA, 1)
+    give_back(YA, 2)
+    give_back(YA, 0)
     pass_on(YA, 4)
     pass_on(ZB, 2)
+    give_back(YB, 5)
+    give_back(YB, 7)
+    give_back(YB, 6)
     pass_on(YA, 3)
     pass_on(ZA, 1)
-    for i in (5, 7, 6):
-        give_back(YB, i)
+    give_back(YB, 3)
+    give_back(YB, 4)
     pass_on(YA, 2)
     pass_on(ZB, 1)
+    give_back(YB, 1)
+    give_back(YB, 2)
+    give_back(YB, 0)
     pass_on(YA, 1)
     finish_z(ZA)
-    for i in (3, 4, 1, 2, 0):
-        give_back(YB, i)
     finish_y(YA)
     pass_on(YB, 4)
     pass_on(YB, 3)
@@ -458,12 +482,10 @@
     gathered(YA)
     gradient(YA)
     finish_z_pooled(ZB)
+    finish_y(YB)
     gathered(ZA)
     gradient(ZA)
-    finish_y(YB)
-    project(YA, first=True)
-    project(ZA)
-    for b in list(bands(YA)) + list(bands(ZA)):
+    for b in bands(YA):
         gather_band(b)
     relay(ZB)
     relay(YB)
@@ -471,10 +493,16 @@
     gradient(ZB)
     gathered(YB)
     gradient(YB)
+    for b in bands(ZA):
+        gather_band(b)
+    project(YA, first=True)
+    project(ZA)
+    for b in bands(ZB):
+        gather_band(b)
+    for b in bands(YB):
+        gather_band(b)
     project(ZB)
     project(YB, final=True)
-    for b in list(bands(ZB)) + list(bands(YB)):
-        gather_band(b)
     arrive(summed_in.at[pl.ds(0, NZ - 1)], gz_rs.at[0])
     total = own_sum[...]
     for dz in range(1, NZ):
@@ -486,8 +514,8 @@
     sent(zbuf.at[pl.ds(1, NZ - 1)], Z)
     sent(sbuf, Y)
     sent(bbuf.at[:, pl.ds(CAP, (NY - 1) * CAP)], B)
-    for kind, buf in ((CZ, msg_z), (CY, msg_y)):
-        sent(buf.at[:, :, :, pl.ds(0, 7 * buf.shape[3] // 8)], kind)
+    sent(msg_z.at[:, :, pl.ds(0, 7 * NY * spn // 8)], CZ)
+    sent(zbuf.at[pl.ds(0, 7), pl.ds(0, spn), pl.ds(0, Y_WIDE)], CY)
     sent(fin_out.at[pl.ds(1, NY - 1)], F)
     sent(everyone.at[pl.ds(0, NX - 1)], X)
     sent(everyone.at[pl.ds(0, NX)], S)
@@ -540,13 +568,13 @@
             scratch((NZ, NY * CAP, width), bf),
             scratch((NY * CAP, ff), bf),
             scratch((NZ, NY * CAP, width), bf),
-            scratch((NZ, NY * CAP, 2 * WIDE), bf),
-            scratch((2, NZ // 2, spn, 2 * WIDE), bf),
-            scratch((2, NZ // 2, spn, 2 * WIDE), bf),
-            scratch((2, NZ // 2, NY * spn, 2 * WIDE), bf),
-            scratch((2, NZ // 2, NY * spn, 2 * WIDE), bf),
-            scratch((NY, spn, 2 * WIDE), bf),
-            scratch((NY, spn, 2 * WIDE), bf),
+            scratch((NZ, NY * CAP, Y_WIDE), bf),
+            scratch((2, NZ // 2, spn, Y_WIDE), bf),
+            scratch((2, NZ // 2, spn, Y_WIDE), bf),
+            scratch((2, NZ // 2, NY * spn, Z_WIDE), bf),
+            scratch((2, NZ // 2, NY * spn, Z_WIDE), bf),
+            scratch((NY, spn, Z_WIDE), bf),
+            scratch((NY, spn, Z_WIDE), bf),
             scratch((groups, spn, width), bf),
             scratch((groups, spn, columns), f32),
             scratch((NZ, NY) + packed, bf),

time: 156 us -> 153 us (0.981)
  Pallas kernels: 155 us -> 151 us
    pallas_call x1, Pallas kernels: 153 us -> 149 us  [local(): pl.pallas_call(kernel, out_shape=(jax.ShapeDtypeStruct((groups, spn, colu...]
where the time goes in v4:
time: 153 us; the launch traced here: 152 us
  Pallas kernels  151 us (99%)
    pallas_call x1, Pallas kernels, local(): pl.pallas_call(kernel, out_shape=(jax.ShapeDtypeStruct((groups, spn, colu...  149 us

profile of v4, /device:TPU:2, one launch (start us, length us, event | category | flops | bytes accessed | tf_op | source)
XLA Modules:
  0.0 151.7 jit_solution(7775344399566025941)
XLA Ops:
  0.6 149.3 %shard_map.104 = (bf16[8,64,320]{2,1,0:T(8,128)(2,1)}, f32[64,320]{1,0:T(8,128)}) custom-call(bf16[128,2048]{1,0:T(8,128)(2,1)} %tokens.1, s32[8,4096]{1,0:T(8,128)} %bitcast.4, f32[8,128]{1,0:T(8,128)} %bitcast.5, s32[8,128]{1,0:T(8,128)} %spans.1, bf16[1,2048,768]{2,1,0:T(8,128)(2,1)} %wg_hbm.1, bf16[1,2048,768]{2,1,0:T(8,128)(2,1)} %wu_hbm.1, ...), custom_call_target="tpu_custom_call" | custom-call | tf_op jit(solution)/shard_map/pallas_call | solution.py:543
  149.9 1.8 %shard_map.105 = (bf16[8,64,320]{2,1,0:T(8,128)(2,1)}, f32[64,320]{1,0:T(8,128)}) custom-call(bf16[8,64,320]{2,1,0:T(8,128)(2,1)} %get-tuple-element.4.student_in, f32[64,320]{1,0:T(8,128)} %get-tuple-element.5.grad_in), custom_call_target="tpu_custom_call" | custom-call | tf_op jit(solution)/shard_map/pallas_call | solution.py:605

commit v5 on v4

--- a/solution.py
+++ b/solution.py
@@ -523,9 +523,15 @@
     sent(summed.at[pl.ds(1, NZ - 1)], GZ)
 
 
-def hand_on(student_in, grad_in, student, grad):
-    student[...] = student_in[...]
-    grad[...] = grad_in[...]
+def hand_on(student_in, grad_in, student, grad, sem):
+    copies = [
+        pltpu.make_async_copy(student_in, student, sem.at[0]),
+        pltpu.make_async_copy(grad_in, grad, sem.at[1]),
+    ]
+    for copy in copies:
+        copy.start()
+    for copy in copies:
+        copy.wait()
 
 
 def local(tokens, expert_ids, gate_weights, span_ids, w_gate, w_up, w_down, w_proj, cotangent):
@@ -605,8 +611,9 @@
     return pl.pallas_call(
         hand_on,
         out_shape=[jax.ShapeDtypeStruct(r.shape, r.dtype) for r in results],
-        in_specs=[vmem] * 2,
-        out_specs=[vmem] * 2,
+        in_specs=[hbm] * 2,
+        out_specs=[hbm] * 2,
+        scratch_shapes=[dma((2,))],
     )(*results)
 
 

time: 153 us -> 167 us (1.092)
  Pallas kernels: 151 us -> 165 us
    pallas_call x1, Pallas kernels: 1.82 us -> 16 us  [local(): pl.pallas_call(hand_on, out_shape=[jax.ShapeDtypeStruct(r.shape, r.dtype)...]
where the time goes in v5:
time: 167 us; the launch traced here: 166 us
  Pallas kernels  165 us (99%)
    pallas_call x1, Pallas kernels, local(): pl.pallas_call(kernel, out_shape=(jax.ShapeDtypeStruct((groups, spn, colu...  149 us
    pallas_call x1, Pallas kernels, local(): pl.pallas_call(hand_on, out_shape=[jax.ShapeDtypeStruct(r.shape, r.dtype)...  16 us

profile of v5, /device:TPU:2, one launch (start us, length us, event | category | flops | bytes accessed | tf_op | source)
XLA Modules:
  0.0 166.1 jit_solution(5606264473296297121)
XLA Ops:
  0.6 149.3 %shard_map.104 = (bf16[8,64,320]{2,1,0:T(8,128)(2,1)}, f32[64,320]{1,0:T(8,128)}) custom-call(bf16[128,2048]{1,0:T(8,128)(2,1)} %tokens.1, s32[8,4096]{1,0:T(8,128)} %bitcast.4, f32[8,128]{1,0:T(8,128)} %bitcast.5, s32[8,128]{1,0:T(8,128)} %spans.1, bf16[1,2048,768]{2,1,0:T(8,128)(2,1)} %wg_hbm.1, bf16[1,2048,768]{2,1,0:T(8,128)(2,1)} %wu_hbm.1, ...), custom_call_target="tpu_custom_call" | custom-call | tf_op jit(solution)/shard_map/pallas_call | solution.py:549
  149.9 16.0 %shard_map.105 = (bf16[8,64,320]{2,1,0:T(8,128)(2,1)}, f32[64,320]{1,0:T(8,128)}) custom-call(bf16[8,64,320]{2,1,0:T(8,128)(2,1)} %get-tuple-element.4.student_in, f32[64,320]{1,0:T(8,128)} %get-tuple-element.5.grad_in), custom_call_target="tpu_custom_call" | custom-call | tf_op jit(solution)/shard_map/pallas_call | solution.py:611
